TPU v7x, 256 devices: a whole 4x4x8 slice. The times are simulated.
256 devices in a mesh: space: 32 (over x, z_lo, core), tm: 8 (over z_hi, y).
Axes of the slice: x: 4, y: 4, z: 8 (z_hi: 2, z_lo: 4; z = z_hi * 4 + z_lo), core: 2. Of those that a mesh axis runs over, the one named last changes fastest.
Arguments:
- node_feats: bfloat16 [128, 14336, 128], P('tm', 'space'), may hold values from -6 to 6
- positions: float32 [128, 3, 14336], P('tm', None, 'space'), may hold values from -3 to 3
- neighbours: int32 [128, 448, 8], P('tm', 'space'), may hold values from 0 to 447, as said below
- edge_in: bfloat16 [256, 128], replicated, may hold values from -0.375 to 0.375
- edge_out: bfloat16 [128, 128], replicated, may hold values from -0.5 to 0.5
- edge_params: float32 [3, 128], replicated, may hold values from -3 to 3
- coord_weight: float32 [128], replicated, may hold values from -0.5 to 0.5
- spectral: bfloat16 [2, 64, 128, 128], replicated, may hold values from -0.375 to 0.375
- node_in: bfloat16 [256, 128], replicated, may hold values from -0.375 to 0.375
- node_out: bfloat16 [128, 128], replicated, may hold values from -0.5 to 0.5
- node_bias: float32 [2, 128], replicated, may hold values from -3 to 3
Outputs:
- new_feats: bfloat16 [128, 14336, 128], P('tm', 'space')
- new_positions: float32 [128, 3, 14336], P('tm', None, 'space')
Inputs may be any that keep to these rules, and one draw needn't show every extreme that they name: neighbours[f, b, s] = (b + o) mod 448 for an offset o with -6 <= o <= 6; the offsets of a block's list may repeat, and every list holds the offsets 0, -6 and +6 in some slots.
All inputs are finite; a program needn't handle non-finite values.
Results may differ from a plain program's by a relative error of at most 0.0065.
Values may be sent and summed in bfloat16 or wider, within the bound.
A program may use at most 128 MiB of HBM per device.

v0:
```python
import math

import jax
import jax.numpy as jnp
from jax import lax
from jax.sharding import PartitionSpec as P

BLOCK = 32
GHOST = 6


def with_halo(block, sides, width):
    for axis, dim in sides:
        count = lax.axis_size(axis)
        forward = [(i, i + 1) for i in range(count - 1)]
        forward.append((count - 1, 0))
        backward = [(target, source) for source, target in forward]
        low = lax.ppermute(
            lax.slice_in_dim(block, block.shape[dim] - width, None, axis=dim), axis, forward
        )
        high = lax.ppermute(lax.slice_in_dim(block, 0, width, axis=dim), axis, backward)
        block = jnp.concatenate([low, block, high], axis=dim)
    return block


def split_parts(values):
    high_part = values.astype(jnp.bfloat16)
    low_part = (values - high_part.astype(jnp.float32)).astype(jnp.bfloat16)
    return (high_part, low_part)


def edge_pass(own_src, other_dst, own_pos, other_pos, picked, edge_out, edge_params, coord_weight):
    frames, own_blocks, block_len, feat_width = own_src.shape
    other_blocks = other_dst.shape[1]
    flat_dst = other_dst.reshape(frames, other_blocks, block_len * feat_width)
    dst_high, dst_low = split_parts(flat_dst)
    block_ids = jnp.arange(other_blocks, dtype=jnp.int32)
    summed = jnp.zeros(own_src.shape, jnp.float32)
    moved = jnp.zeros(own_pos.shape, jnp.float32)
    for slot_num in range(picked.shape[2]):
        chosen = picked[:, :, slot_num]
        select_f32 = (chosen[:, :, None] == block_ids[None, None, :]).astype(jnp.float32)
        select_bf = select_f32.astype(jnp.bfloat16)
        near_dst = jnp.einsum(
            "fbc,fcx->fbx", select_bf, dst_high, preferred_element_type=jnp.float32
        ) + jnp.einsum("fbc,fcx->fbx", select_bf, dst_low, preferred_element_type=jnp.float32)
        near_dst = near_dst.reshape(own_src.shape)
        near_pos = jnp.einsum(
            "fbc,fdcl->fdbl", select_f32, other_pos, precision=lax.Precision.HIGHEST
        )
        offset_vec = own_pos - near_pos
        dist_sq = jnp.sum(offset_vec * offset_vec, axis=1)
        pre_act = own_src + near_dst + edge_params[0] + dist_sq[..., None] * edge_params[1]
        hidden = jax.nn.silu(pre_act).astype(jnp.bfloat16)
        out_act = (
            jnp.dot(
                hidden.reshape(-1, feat_width), edge_out, preferred_element_type=jnp.float32
            ).reshape(pre_act.shape)
            + edge_params[2]
        )
        message = jax.nn.silu(out_act)
        summed = summed + message
        weight = jnp.sum(message * coord_weight, axis=-1) / (1.0 + jnp.sqrt(dist_sq + 1.0))
        moved = moved + offset_vec * weight[:, None]
    return (summed, moved)


def spectral_conv(msg_block, spectral, out_count):
    frame_count, item_count, feat_width = msg_block.shape
    mode_count = spectral.shape[1]
    mode_ids = jnp.arange(mode_count, dtype=jnp.int32)
    time_ids = jnp.arange(frame_count, dtype=jnp.int32)
    step_angle = 2.0 * math.pi / frame_count
    angles = (mode_ids[:, None] * time_ids[None, :] % frame_count).astype(jnp.float32) * step_angle
    forward = jnp.concatenate([jnp.cos(angles), -jnp.sin(angles)], axis=0)
    fwd_high, fwd_low = split_parts(forward)
    flat_msg = msg_block.reshape(frame_count, -1)
    coeffs = jnp.dot(fwd_high, flat_msg, preferred_element_type=jnp.float32) + jnp.dot(
        fwd_low, flat_msg, preferred_element_type=jnp.float32
    )
    coeffs = coeffs.astype(jnp.bfloat16).reshape(2, mode_count, item_count, feat_width)
    mixed_real = jnp.einsum(
        "knh,khg->kng", coeffs[0], spectral[0], preferred_element_type=jnp.float32
    ) - jnp.einsum("knh,khg->kng", coeffs[1], spectral[1], preferred_element_type=jnp.float32)
    mixed_imag = jnp.einsum(
        "knh,khg->kng", coeffs[0], spectral[1], preferred_element_type=jnp.float32
    ) + jnp.einsum("knh,khg->kng", coeffs[1], spectral[0], preferred_element_type=jnp.float32)
    out_times = jnp.arange(out_count, dtype=jnp.int32)
    back_angles = (out_times[:, None] * mode_ids[None, :] % frame_count).astype(
        jnp.float32
    ) * step_angle
    weights = (jnp.where(mode_ids == 0, 1.0, 2.0) / frame_count).astype(jnp.float32)
    inverse = jnp.concatenate(
        [jnp.cos(back_angles) * weights, -jnp.sin(back_angles) * weights], axis=1
    )
    inv_high, inv_low = split_parts(inverse)
    mixed_all = jnp.concatenate([mixed_real, mixed_imag], axis=0).reshape(2 * mode_count, -1)
    mix_high, mix_low = split_parts(mixed_all)
    conv_out = (
        jnp.dot(inv_high, mix_high, preferred_element_type=jnp.float32)
        + jnp.dot(inv_low, mix_high, preferred_element_type=jnp.float32)
        + jnp.dot(inv_high, mix_low, preferred_element_type=jnp.float32)
    )
    return conv_out.astype(jnp.bfloat16).reshape(out_count, item_count, feat_width)


def shards(
    node_feats,
    positions,
    neighbours,
    edge_in,
    edge_out,
    edge_params,
    coord_weight,
    spectral,
    node_in,
    node_out,
    node_bias,
):
    frames, local_rows, feat_width = node_feats.shape
    blocks = local_rows // BLOCK
    rim_rows = GHOST * BLOCK
    slot_count = neighbours.shape[2]
    slab_index = lax.axis_index("space")
    total_blocks = blocks * lax.axis_size("space")
    first_block = slab_index * blocks - GHOST
    ext_feats = with_halo(node_feats, (("space", 1),), rim_rows)
    ext_pos = with_halo(positions.astype(jnp.bfloat16), (("space", 2),), rim_rows).astype(
        positions.dtype
    )
    ext_pos4 = ext_pos.reshape(frames, 3, blocks + 2 * GHOST, BLOCK)
    own_src = jnp.dot(node_feats, edge_in[:feat_width], preferred_element_type=jnp.float32).reshape(
        frames, blocks, BLOCK, feat_width
    )
    own_pos = positions.reshape(frames, 3, blocks, BLOCK)
    picked = (neighbours - first_block) % total_blocks
    ext_dst = jnp.dot(ext_feats, edge_in[feat_width:], preferred_element_type=jnp.float32).reshape(
        frames, blocks + 2 * GHOST, BLOCK, feat_width
    )
    summed, moved = edge_pass(
        own_src, ext_dst, own_pos, ext_pos4, picked, edge_out, edge_params, coord_weight
    )
    mean_msg = (summed / slot_count).astype(jnp.bfloat16).reshape(frames, local_rows, feat_width)
    new_positions = positions + (moved / slot_count).reshape(frames, 3, local_rows)
    regrouped = lax.all_to_all(mean_msg, "tm", split_axis=1, concat_axis=0, tiled=True)
    conv_all = spectral_conv(regrouped, spectral, regrouped.shape[0])
    conv_own = lax.all_to_all(conv_all, "tm", split_axis=0, concat_axis=1, tiled=True)
    node_pre = (
        jnp.dot(node_feats, node_in[:feat_width], preferred_element_type=jnp.float32)
        + jnp.dot(conv_own, node_in[feat_width:], preferred_element_type=jnp.float32)
        + node_bias[0]
    )
    node_hidden = jax.nn.silu(node_pre).astype(jnp.bfloat16)
    new_feats = (
        node_feats.astype(jnp.float32)
        + (jnp.dot(node_hidden, node_out, preferred_element_type=jnp.float32) + node_bias[1])
    ).astype(jnp.bfloat16)
    return (new_feats, new_positions)


def solution(mesh):
    placed = (
        P("tm", "space", None),
        P("tm", None, "space"),
        P("tm", "space", None),
        P(),
        P(),
        P(),
        P(),
        P(),
        P(),
        P(),
        P(),
    )
    return jax.shard_map(
        shards,
        mesh=mesh,
        in_specs=placed,
        out_specs=(P("tm", "space", None), P("tm", None, "space")),
        check_vma=False,
    )
```

profile of v0, /device:TPU:38, one launch (start us, length us, event | category | flops | bytes accessed | tf_op | source)
XLA Modules:
  0.0 346.9 jit_solution(16150701191727364065)
XLA Ops:
  12.7 8.2 %collective-permute-done.2 = bf16[16,3,192]{2,0,1:T(8,128)(2,1)S(1)} collective-permute-done((bf16[16,3,192]{2,0,1:T(8,128)(2,1)S(1)}, bf16[16,3,192]{2,0,1:T(8,128)(2,1)S(1)}, u32[]{:S(2)}, u32[]{:S(2)}) %collective-permute-start.2) | collective-permute-done | bytes 18464 | tf_op jit(solution)/shard_map/ppermute | solution.py:18
  39.9 5.0 %fusion.3 = f32[16,832,128]{2,1,0:T(8,128)} fusion(bf16[16,192,128]{2,1,0:T(8,128)(2,1)} %collective-permute-done.1, bf16[16,448,128]{2,1,0:T(8,128)(2,1)S(1)} %copy-done.2, bf16[16,192,128]{2,1,0:T(8,128)(2,1)S(1)} %collective-permute-done, bf16[256,128]{1,0:T(8,128)(2,1)S(1)} %copy-done.41), kind=kOutput, calls=%fused_computation.45 | convolution fusion | flops 446431232 | bytes 10256384 | tf_op jit(solution)/shard_map/dot_general | solution.py:137
  44.9 8.5 %reshape_reshape.3 = f32[16,26,4096]{2,1,0:T(8,128)} reshape(f32[16,832,128]{2,1,0:T(8,128)} %fusion.3) | data formatting | bytes 13631488 | tf_op jit(solution)/shard_map/reshape;reshape | solution.py:35
  53.4 8.1 %subtract_convert_fusion = (bf16[16,26,4096]{2,1,0:T(8,128)(2,1)S(1)}, bf16[16,26,4096]{2,1,0:T(8,128)(2,1)S(1)}) fusion(f32[16,26,4096]{2,1,0:T(8,128)} %reshape_reshape.3), kind=kLoop, calls=%fused_computation.5 | loop fusion | flops 6815744 | bytes 13631488 | tf_op jit(solution)/shard_map/convert_element_type | solution.py:28
  84.7 5.2 %reshape.371 = f32[16,14,32,128]{3,2,1,0:T(8,128)} reshape(f32[16,14,4096]{2,1,0:T(8,128)} %convolution_add_fusion.3) | data formatting | bytes 7340032 | tf_op jit(solution)/shard_map/reshape | solution.py:47
  89.9 6.2 %convolution_add_fusion.4 = f32[16,14,4096]{2,1,0:T(8,128)} fusion(f32[16,14,4096]{2,1,0:T(8,128)} %fusion.67, bf16[16,26,4096]{2,1,0:T(8,128)(2,1)} %copy-done.1, s32[16,14]{1,0:T(8,128)S(1)} %copy-done.38), kind=kOutput, calls=%fused_computation.7 | convolution fusion | flops 48645184 | bytes 10748800 | tf_op jit(solution)/shard_map/fbc,fcx->fbx/dot_general | solution.py:46
  96.2 5.3 %reshape.370 = f32[16,14,32,128]{3,2,1,0:T(8,128)} reshape(f32[16,14,4096]{2,1,0:T(8,128)} %convolution_add_fusion.4) | data formatting | bytes 7340032 | tf_op jit(solution)/shard_map/reshape | solution.py:47
  101.5 6.3 %convolution_add_fusion.5 = f32[16,14,4096]{2,1,0:T(8,128)} fusion(f32[16,14,4096]{2,1,0:T(8,128)} %fusion.66, bf16[16,26,4096]{2,1,0:T(8,128)(2,1)} %copy-done.1, s32[16,14]{1,0:T(8,128)S(1)} %copy-done.37), kind=kOutput, calls=%fused_computation.8 | convolution fusion | flops 48645184 | bytes 10748800 | tf_op jit(solution)/shard_map/fbc,fcx->fbx/dot_general | solution.py:46
  107.7 5.4 %reshape.369 = f32[16,14,32,128]{3,2,1,0:T(8,128)} reshape(f32[16,14,4096]{2,1,0:T(8,128)} %convolution_add_fusion.5) | data formatting | bytes 7340032 | tf_op jit(solution)/shard_map/reshape | solution.py:47
  113.1 6.3 %convolution_add_fusion.6 = f32[16,14,4096]{2,1,0:T(8,128)} fusion(f32[16,14,4096]{2,1,0:T(8,128)} %fusion.65, bf16[16,26,4096]{2,1,0:T(8,128)(2,1)} %copy-done.1, s32[16,14]{1,0:T(8,128)S(1)} %copy-done.36), kind=kOutput, calls=%fused_computation.9 | convolution fusion | flops 48645184 | bytes 10748800 | tf_op jit(solution)/shard_map/fbc,fcx->fbx/dot_general | solution.py:46
  119.4 5.2 %reshape.368 = f32[16,14,32,128]{3,2,1,0:T(8,128)} reshape(f32[16,14,4096]{2,1,0:T(8,128)} %convolution_add_fusion.6) | data formatting | bytes 7340032 | tf_op jit(solution)/shard_map/reshape | solution.py:47
  124.7 6.2 %convolution_add_fusion.7 = f32[16,14,4096]{2,1,0:T(8,128)} fusion(f32[16,14,4096]{2,1,0:T(8,128)} %fusion.64, bf16[16,26,4096]{2,1,0:T(8,128)(2,1)} %copy-done.1, s32[16,14]{1,0:T(8,128)S(1)} %copy-done.35), kind=kOutput, calls=%fused_computation.10 | convolution fusion | flops 48645184 | bytes 10748800 | tf_op jit(solution)/shard_map/fbc,fcx->fbx/dot_general | solution.py:46
  130.9 5.3 %reshape.367 = f32[16,14,32,128]{3,2,1,0:T(8,128)} reshape(f32[16,14,4096]{2,1,0:T(8,128)} %convolution_add_fusion.7) | data formatting | bytes 7340032 | tf_op jit(solution)/shard_map/reshape | solution.py:47
  136.2 6.2 %convolution_add_fusion.8 = f32[16,14,4096]{2,1,0:T(8,128)} fusion(f32[16,14,4096]{2,1,0:T(8,128)} %fusion.63, bf16[16,26,4096]{2,1,0:T(8,128)(2,1)} %copy-done.1, s32[16,14]{1,0:T(8,128)S(1)} %get-tuple-element.23), kind=kOutput, calls=%fused_computation.11 | convolution fusion | flops 48645184 | bytes 10748800 | tf_op jit(solution)/shard_map/fbc,fcx->fbx/dot_general | solution.py:46
  142.4 5.2 %reshape.366 = f32[16,14,32,128]{3,2,1,0:T(8,128)} reshape(f32[16,14,4096]{2,1,0:T(8,128)} %convolution_add_fusion.8) | data formatting | bytes 7340032 | tf_op jit(solution)/shard_map/reshape | solution.py:47
  147.6 6.3 %convolution_add_fusion.9 = f32[16,14,4096]{2,1,0:T(8,128)} fusion(f32[16,14,4096]{2,1,0:T(8,128)} %fusion.62, bf16[16,26,4096]{2,1,0:T(8,128)(2,1)} %copy-done.1, s32[16,14]{1,0:T(8,128)S(1)} %get-tuple-element.17), kind=kOutput, calls=%fused_computation.12 | convolution fusion | flops 48645184 | bytes 10748800 | tf_op jit(solution)/shard_map/fbc,fcx->fbx/dot_general | solution.py:46
  153.9 5.3 %reshape.365 = f32[16,14,32,128]{3,2,1,0:T(8,128)} reshape(f32[16,14,4096]{2,1,0:T(8,128)} %convolution_add_fusion.9) | data formatting | bytes 7340032 | tf_op jit(solution)/shard_map/reshape | solution.py:47
  159.2 6.3 %convolution_add_fusion.10 = f32[16,14,4096]{2,1,0:T(8,128)} fusion(f32[16,14,4096]{2,1,0:T(8,128)} %fusion.61, bf16[16,26,4096]{2,1,0:T(8,128)(2,1)} %copy-done.1, s32[16,14]{1,0:T(8,128)S(1)} %get-tuple-element.24), kind=kOutput, calls=%fused_computation.13 | convolution fusion | flops 48645184 | bytes 10748800 | tf_op jit(solution)/shard_map/fbc,fcx->fbx/dot_general | solution.py:46
  165.5 5.3 %reshape.364 = f32[16,14,32,128]{3,2,1,0:T(8,128)} reshape(f32[16,14,4096]{2,1,0:T(8,128)} %convolution_add_fusion.10) | data formatting | bytes 7340032 | tf_op jit(solution)/shard_map/reshape | solution.py:47
  170.8 5.8 %divide_multiply_fusion = f32[16,14,32,128]{3,2,1,0:T(8,128)} fusion(f32[128]{0:T(128)S(1)} %copy-done.45, f32[16,14,32,128]{3,2,1,0:T(8,128)} %bitcast.242, f32[16,14,32,128]{3,2,1,0:T(8,128)} %reshape.371, f32[16,14,32]{2,1,0:T(8,128)S(1)} %copy-done.22, f32[128]{0:T(128)S(1)} %copy-done.46, f32[128]{0:T(128)S(1)} %get-tuple-element.27, ...), kind=kOutput, calls=%fused_computation.29 | convolution fusion | flops 247726080 | bytes 11073024 | tf_op jit(solution)/shard_map/dot_general | solution.py:56
  177.5 3.7 %divide_multiply_fusion.1 = f32[16,14,32,128]{3,2,1,0:T(8,128)} fusion(f32[128]{0:T(128)S(1)} %copy-done.45, f32[16,14,32,128]{3,2,1,0:T(8,128)S(1)} %bitcast.244, f32[16,14,32,128]{3,2,1,0:T(8,128)S(1)} %copy-done.6, f32[16,14,32]{2,1,0:T(8,128)S(1)} %copy-done.23, f32[128]{0:T(128)S(1)} %copy-done.46, f32[128]{0:T(128)S(1)} %get-tuple-element.27, ...), kind=kOutput, calls=%fused_computation.31 | convolution fusion | flops 247726080 | bytes 11073024 | tf_op jit(solution)/shard_map/dot_general | solution.py:56
  181.3 3.8 %divide_multiply_fusion.2 = f32[16,14,32,128]{3,2,1,0:T(8,128)} fusion(f32[128]{0:T(128)S(1)} %copy-done.45, f32[16,14,32,128]{3,2,1,0:T(8,128)S(1)} %bitcast.245, f32[16,14,32,128]{3,2,1,0:T(8,128)S(1)} %copy-done.7, f32[16,14,32]{2,1,0:T(8,128)S(1)} %copy-done.24, f32[128]{0:T(128)S(1)} %copy-done.46, f32[128]{0:T(128)S(1)} %get-tuple-element.27, ...), kind=kOutput, calls=%fused_computation.33 | convolution fusion | flops 247726080 | bytes 11073024 | tf_op jit(solution)/shard_map/dot_general | solution.py:56
  185.0 3.8 %divide_multiply_fusion.3 = f32[16,14,32,128]{3,2,1,0:T(8,128)} fusion(f32[128]{0:T(128)S(1)} %copy-done.45, f32[16,14,32,128]{3,2,1,0:T(8,128)S(1)} %bitcast.246, f32[16,14,32,128]{3,2,1,0:T(8,128)S(1)} %copy-done.8, f32[16,14,32]{2,1,0:T(8,128)S(1)} %copy-done.25, f32[128]{0:T(128)S(1)} %copy-done.46, f32[128]{0:T(128)S(1)} %get-tuple-element.27, ...), kind=kOutput, calls=%fused_computation.35 | convolution fusion | flops 247726080 | bytes 11073024 | tf_op jit(solution)/shard_map/dot_general | solution.py:56
  188.8 3.8 %divide_multiply_fusion.4 = f32[16,14,32,128]{3,2,1,0:T(8,128)} fusion(f32[128]{0:T(128)S(1)} %copy-done.45, f32[16,14,32,128]{3,2,1,0:T(8,128)S(1)} %bitcast.247, f32[16,14,32,128]{3,2,1,0:T(8,128)S(1)} %copy-done.9, f32[16,14,32]{2,1,0:T(8,128)S(1)} %copy-done.26, f32[128]{0:T(128)S(1)} %copy-done.46, f32[128]{0:T(128)S(1)} %get-tuple-element.27, ...), kind=kOutput, calls=%fused_computation.37 | convolution fusion | flops 247726080 | bytes 11073024 | tf_op jit(solution)/shard_map/dot_general | solution.py:56
  192.6 3.8 %divide_multiply_fusion.5 = f32[16,14,32,128]{3,2,1,0:T(8,128)} fusion(f32[128]{0:T(128)S(1)} %copy-done.45, f32[16,14,32,128]{3,2,1,0:T(8,128)S(1)} %bitcast.248, f32[16,14,32,128]{3,2,1,0:T(8,128)S(1)} %copy-done.10, f32[16,14,32]{2,1,0:T(8,128)S(1)} %copy-done.27, f32[128]{0:T(128)S(1)} %copy-done.46, f32[128]{0:T(128)S(1)} %get-tuple-element.27, ...), kind=kOutput, calls=%fused_computation.39 | convolution fusion | flops 247726080 | bytes 11073024 | tf_op jit(solution)/shard_map/dot_general | solution.py:56
  196.5 3.8 %divide_multiply_fusion.6 = f32[16,14,32,128]{3,2,1,0:T(8,128)} fusion(f32[128]{0:T(128)S(1)} %copy-done.45, f32[16,14,32,128]{3,2,1,0:T(8,128)S(1)} %bitcast.249, f32[16,14,32,128]{3,2,1,0:T(8,128)S(1)} %copy-done.11, f32[16,14,32]{2,1,0:T(8,128)S(1)} %copy-done.28, f32[128]{0:T(128)S(1)} %copy-done.46, f32[128]{0:T(128)S(1)} %get-tuple-element.27, ...), kind=kOutput, calls=%fused_computation.41 | convolution fusion | flops 247726080 | bytes 11073024 | tf_op jit(solution)/shard_map/dot_general | solution.py:56
  200.3 16.8 %multiply_reduce_fusion.7 = (f32[16,14,32]{2,1,0:T(8,128)}, f32[16,14,32]{2,1,0:T(8,128)}, f32[16,14,32]{2,1,0:T(8,128)}, f32[16,14,32]{2,1,0:T(8,128)}, f32[16,...) fusion(f32[128]{0:T(128)S(1)} %copy-done.48, ...), kind=kOutput, calls=%fused_computation.25 | convolution fusion | flops 270606336 | bytes 35158016 | tf_op jit(solution)/shard_map/dot_general | solution.py:56
  219.5 10.3 %all-to-all-start = ((bf16[16,448,128]{2,0,1:T(8,128)(2,1)}), bf16[16,448,128]{2,0,1:T(8,128)(2,1)S(1)}, u32[]{:S(2)}, u32[]{:S(2)}) async-start(bf16[16,448,128]{2,0,1:T(8,128)(2,1)} %copy.167), calls=%async_computation | async-start | bytes 3670016 | tf_op jit(solution)/shard_map/all_to_all | solution.py:145
  230.1 46.1 %all-to-all-done = bf16[16,448,128]{2,0,1:T(8,128)(2,1)S(1)} async-done(((bf16[16,448,128]{2,0,1:T(8,128)(2,1)}), bf16[16,448,128]{2,0,1:T(8,128)(2,1)S(1)}, u32[]{:S(2)}, u32[]{:S(2)}) %all-to-all-start) | async-done | bytes 1835040 | tf_op jit(solution)/shard_map/all_to_all | solution.py:145
  287.8 4.8 %all-to-all-start.1 = ((bf16[128,56,128]{2,1,0:T(8,128)(2,1)}), bf16[128,56,128]{2,1,0:T(8,128)(2,1)}, u32[]{:S(2)}, u32[]{:S(2)}) async-start(bf16[128,56,128]{2,1,0:T(8,128)(2,1)} %bitcast.240), calls=%async_computation.1 | async-start | bytes 3670016 | tf_op jit(solution)/shard_map/all_to_all | solution.py:147
  297.1 40.9 %all-to-all-done.1 = bf16[128,56,128]{2,1,0:T(8,128)(2,1)} async-done(((bf16[128,56,128]{2,1,0:T(8,128)(2,1)}), bf16[128,56,128]{2,1,0:T(8,128)(2,1)}, u32[]{:S(2)}, u32[]{:S(2)}) %all-to-all-start.1) | async-done | bytes 1835040 | tf_op jit(solution)/shard_map/all_to_all | solution.py:147
  341.1 5.4 %add_convert_fusion = bf16[16,448,128]{2,1,0:T(8,128)(2,1)} fusion(bf16[16,448,128]{2,1,0:T(8,128)(2,1)S(1)} %copy-done.3, f32[128]{0:T(128)S(1)} %get-tuple-element.31, f32[16,448,128]{2,1,0:T(8,128)} %fusion.124, bf16[16,448,128]{2,1,0:T(8,128)(2,1)} %bitcast.251, f32[128]{0:T(128)S(1)} %get-tuple-element.30, bf16[128,128]{1,0:T(8,128)(2,1)S(1)} %copy-done.47, ...), kind=kOutput, calls=%fused_computation.26 | convolution fusion | flops 479854592 | bytes 9241600 | tf_op jit(solution)/shard_map/dot_general | solution.py:156
  (162 shorter events, 76.5 us)
Async XLA Ops:
  0.6 170.1 %copy-start = (bf16[128,128]{1,0:T(8,128)(2,1)S(1)}, bf16[128,128]{1,0:T(8,128)(2,1)}, u32[]{:S(2)}) copy-start(bf16[128,128]{1,0:T(8,128)(2,1)} %param.15) | copy-start | bytes 98308
  0.6 8.9 %copy-start.2 = (bf16[16,448,128]{2,1,0:T(8,128)(2,1)S(1)}, bf16[16,448,128]{2,1,0:T(8,128)(2,1)}, u32[]{:S(2)}) copy-start(bf16[16,448,128]{2,1,0:T(8,128)(2,1)} %param.11) | copy-start | bytes 5505028
  0.7 8.9 %copy-start.40 = (bf16[256,128]{1,0:T(8,128)(2,1)S(1)}, bf16[256,128]{1,0:T(8,128)(2,1)}, u32[]{:S(2)}) copy-start(bf16[256,128]{1,0:T(8,128)(2,1)} %param.14) | copy-start | bytes 196612
  3.5 8.5 %copy-start.43 = (f32[3,128]{1,0:T(4,128)S(1)}, f32[3,128]{1,0:T(4,128)}, u32[]{:S(2)}) copy-start(f32[3,128]{1,0:T(4,128)} %param.16) | copy-start | bytes 4612
  3.5 9.1 %copy-start.20 = (f32[16,3,448]{2,0,1:T(8,128)S(1)}, f32[16,3,448]{2,0,1:T(8,128)}, u32[]{:S(2)}) copy-start(f32[16,3,448]{2,0,1:T(8,128)} %param.12) | copy-start | bytes 258052
  3.5 36.4 %collective-permute-start = (bf16[16,192,128]{2,1,0:T(8,128)(2,1)}, bf16[16,192,128]{2,1,0:T(8,128)(2,1)S(1)}, u32[]{:S(2)}, u32[]{:S(2)}) collective-permute-start(bf16[16,192,128]{2,1,0:T(8,128)(2,1)} %get-tuple-element.15), channel_id=1, source_target_pairs={{0,8},{8,16},{16,24},{24,32},{32,40},{40,48},{48,56},{56,64},{64,7... | collective-permute-start | bytes 2359304 | tf_op jit(solution)/shard_map/ppermute | solution.py:18
  3.5 36.4 %collective-permute-start.1 = (bf16[16,192,128]{2,1,0:T(8,128)(2,1)}, bf16[16,192,128]{2,1,0:T(8,128)(2,1)}, u32[]{:S(2)}, u32[]{:S(2)}) collective-permute-start(bf16[16,192,128]{2,1,0:T(8,128)(2,1)} %get-tuple-element.16), channel_id=1, source_target_pairs={{8,0},{16,8},{24,16},{32,24},{40,32},{48,40},{56,48},{64,56},{72,6... | collective-permute-start | bytes 2359304 | tf_op jit(solution)/shard_map/ppermute | solution.py:21
  6.1 14.8 %collective-permute-start.2 = (bf16[16,3,192]{2,0,1:T(8,128)(2,1)S(1)}, bf16[16,3,192]{2,0,1:T(8,128)(2,1)S(1)}, u32[]{:S(2)}, u32[]{:S(2)}) collective-permute-start(bf16[16,3,192]{2,0,1:T(8,128)(2,1)S(1)} %get-tuple-element.25), channel_id=1, source_target_pairs={{0,8},{8,16},{16,24},{24,32},{32,40},{40,48},{48,56},{56,64},{64,7... | collective-permute-start | bytes 55304 | tf_op jit(solution)/shard_map/ppermute | solution.py:18
  6.5 17.4 %collective-permute-start.3 = (bf16[16,3,192]{2,0,1:T(8,128)(2,1)S(1)}, bf16[16,3,192]{2,0,1:T(8,128)(2,1)S(1)}, u32[]{:S(2)}, u32[]{:S(2)}) collective-permute-start(bf16[16,3,192]{2,0,1:T(8,128)(2,1)S(1)} %get-tuple-element.26), channel_id=1, source_target_pairs={{8,0},{16,8},{24,16},{32,24},{40,32},{48,40},{56,48},{64,56},{72,6... | collective-permute-start | bytes 55304 | tf_op jit(solution)/shard_map/ppermute | solution.py:21
  24.3 7.1 %copy-start.36 = (s32[16,14]{1,0:T(8,128)S(1)}, s32[16,14]{1,0:T(8,128)}, u32[]{:S(2)}) copy-start(s32[16,14]{1,0:T(8,128)} %get-tuple-element.21) | copy-start | bytes 2692
  24.4 8.8 %copy-start.35 = (s32[16,14]{1,0:T(8,128)S(1)}, s32[16,14]{1,0:T(8,128)}, u32[]{:S(2)}) copy-start(s32[16,14]{1,0:T(8,128)} %get-tuple-element.22) | copy-start | bytes 2692
  29.1 10.8 %copy-start.41 = (bf16[256,128]{1,0:T(8,128)(2,1)S(1)}, bf16[256,128]{1,0:T(8,128)(2,1)}, u32[]{:S(2)}) copy-start(bf16[256,128]{1,0:T(8,128)(2,1)} %param.14) | copy-start | bytes 196612
  53.4 8.2 %copy-start.39 = (s32[16,14]{1,0:T(8,128)S(1)}, s32[16,14]{1,0:T(8,128)}, u32[]{:S(2)}) copy-start(s32[16,14]{1,0:T(8,128)} %get-tuple-element.18) | copy-start | bytes 2692
  61.5 20.1 %copy-start.1 = (bf16[16,26,4096]{2,1,0:T(8,128)(2,1)}, bf16[16,26,4096]{2,1,0:T(8,128)(2,1)S(1)}, u32[]{:S(2)}) copy-start(bf16[16,26,4096]{2,1,0:T(8,128)(2,1)S(1)} %get-tuple-element.10) | copy-start | bytes 10223620
  165.5 5.3 %copy-start.22 = (f32[16,14,32]{2,1,0:T(8,128)S(1)}, f32[16,14,32]{2,1,0:T(8,128)}, u32[]{:S(2)}) copy-start(f32[16,14,32]{2,1,0:T(8,128)} %get-tuple-element.48) | copy-start | bytes 86020
  165.5 5.3 %copy-start.45 = (f32[128]{0:T(128)S(1)}, f32[128]{0:T(128)}, u32[]{:S(2)}) copy-start(f32[128]{0:T(128)} %get-tuple-element.28) | copy-start | bytes 1540
  165.5 5.3 %copy-start.46 = (f32[128]{0:T(128)S(1)}, f32[128]{0:T(128)}, u32[]{:S(2)}) copy-start(f32[128]{0:T(128)} %get-tuple-element.29) | copy-start | bytes 1540
  170.8 5.8 %copy-start.5 = (f32[16,448,128]{2,1,0:T(8,128)S(1)}, f32[16,448,128]{2,1,0:T(8,128)}, u32[]{:S(2)}) copy-start(f32[16,448,128]{2,1,0:T(8,128)} %fusion.122) | copy-start | bytes 11010052
  170.8 6.7 %copy-start.6 = (f32[16,14,32,128]{3,2,1,0:T(8,128)S(1)}, f32[16,14,32,128]{3,2,1,0:T(8,128)}, u32[]{:S(2)}) copy-start(f32[16,14,32,128]{3,2,1,0:T(8,128)} %reshape.370) | copy-start | bytes 11010052
  170.8 6.7 %copy-start.23 = (f32[16,14,32]{2,1,0:T(8,128)S(1)}, f32[16,14,32]{2,1,0:T(8,128)}, u32[]{:S(2)}) copy-start(f32[16,14,32]{2,1,0:T(8,128)} %get-tuple-element.46) | copy-start | bytes 86020
  181.2 3.8 %copy-start.8 = (f32[16,14,32,128]{3,2,1,0:T(8,128)S(1)}, f32[16,14,32,128]{3,2,1,0:T(8,128)}, u32[]{:S(2)}) copy-start(f32[16,14,32,128]{3,2,1,0:T(8,128)} %reshape.368) | copy-start | bytes 11010052
  181.2 3.8 %copy-start.25 = (f32[16,14,32]{2,1,0:T(8,128)S(1)}, f32[16,14,32]{2,1,0:T(8,128)}, u32[]{:S(2)}) copy-start(f32[16,14,32]{2,1,0:T(8,128)} %get-tuple-element.42) | copy-start | bytes 86020
  188.8 3.8 %copy-start.10 = (f32[16,14,32,128]{3,2,1,0:T(8,128)S(1)}, f32[16,14,32,128]{3,2,1,0:T(8,128)}, u32[]{:S(2)}) copy-start(f32[16,14,32,128]{3,2,1,0:T(8,128)} %reshape.366) | copy-start | bytes 11010052
  188.8 3.8 %copy-start.27 = (f32[16,14,32]{2,1,0:T(8,128)S(1)}, f32[16,14,32]{2,1,0:T(8,128)}, u32[]{:S(2)}) copy-start(f32[16,14,32]{2,1,0:T(8,128)} %get-tuple-element.38) | copy-start | bytes 86020
  192.6 3.9 %copy-start.11 = (f32[16,14,32,128]{3,2,1,0:T(8,128)S(1)}, f32[16,14,32,128]{3,2,1,0:T(8,128)}, u32[]{:S(2)}) copy-start(f32[16,14,32,128]{3,2,1,0:T(8,128)} %reshape.365) | copy-start | bytes 11010052
  192.6 3.9 %copy-start.28 = (f32[16,14,32]{2,1,0:T(8,128)S(1)}, f32[16,14,32]{2,1,0:T(8,128)}, u32[]{:S(2)}) copy-start(f32[16,14,32]{2,1,0:T(8,128)} %get-tuple-element.36) | copy-start | bytes 86020
  219.5 56.8 %all-to-all-start = ((bf16[16,448,128]{2,0,1:T(8,128)(2,1)}), bf16[16,448,128]{2,0,1:T(8,128)(2,1)S(1)}, u32[]{:S(2)}, u32[]{:S(2)}) async-start(bf16[16,448,128]{2,0,1:T(8,128)(2,1)} %copy.167), calls=%async_computation | async-start | bytes 3670016 | tf_op jit(solution)/shard_map/all_to_all | solution.py:145
  286.2 6.4 %copy-start.44 = (f32[2,128]{1,0:T(2,128)S(1)}, f32[2,128]{1,0:T(2,128)}, u32[]{:S(2)}) copy-start(f32[2,128]{1,0:T(2,128)} %param.21) | copy-start | bytes 3076
  286.2 6.5 %copy-start.3 = (bf16[16,448,128]{2,1,0:T(8,128)(2,1)S(1)}, bf16[16,448,128]{2,1,0:T(8,128)(2,1)}, u32[]{:S(2)}) copy-start(bf16[16,448,128]{2,1,0:T(8,128)(2,1)} %param.11) | copy-start | bytes 5505028
  286.2 6.5 %copy-start.42 = (bf16[256,128]{1,0:T(8,128)(2,1)S(1)}, bf16[256,128]{1,0:T(8,128)(2,1)}, u32[]{:S(2)}) copy-start(bf16[256,128]{1,0:T(8,128)(2,1)} %param.19) | copy-start | bytes 196612
  287.8 50.2 %all-to-all-start.1 = ((bf16[128,56,128]{2,1,0:T(8,128)(2,1)}), bf16[128,56,128]{2,1,0:T(8,128)(2,1)}, u32[]{:S(2)}, u32[]{:S(2)}) async-start(bf16[128,56,128]{2,1,0:T(8,128)(2,1)} %bitcast.240), calls=%async_computation.1 | async-start | bytes 3670016 | tf_op jit(solution)/shard_map/all_to_all | solution.py:147
  295.8 45.3 %copy-start.47 = (bf16[128,128]{1,0:T(8,128)(2,1)S(1)}, bf16[128,128]{1,0:T(8,128)(2,1)}, u32[]{:S(2)}) copy-start(bf16[128,128]{1,0:T(8,128)(2,1)} %param.20) | copy-start | bytes 98308
  (23 other events, 66.5 us)
where the time goes:
time: 353 us; the launch traced here: 347 us
  matrix products  150 us (42%)
  waiting for transfers between devices  98.3 us (28%)
  local copies, waits for them, and re-layouts  67.2 us (19%)
  starting transfers between devices  18.7 us (5%)
  other arithmetic  11.2 us (3%)
    dot_general x8, matrix products, edge_pass(): jnp.einsum('fbc,fcx->fbx', select_bf, dst_low, preferred_element_type=jnp...  46.9 us
    all_to_all x1, waiting for transfers between devices, shards(): lax.all_to_all(mean_msg, 'tm', split_axis=1, concat_axis=0, tiled=True)  46.1 us
    dot_general x8, matrix products, edge_pass(): jnp.dot(hidden.reshape(-1, feat_width), edge_out, preferred_element_type=...  45.3 us
    reshape x8, local copies, waits for them, and re-layouts, edge_pass(): near_dst = near_dst.reshape(own_src.shape)  42.3 us
    all_to_all x1, waiting for transfers between devices, shards(): lax.all_to_all(conv_all, 'tm', split_axis=0, concat_axis=1, tiled=True)  40.9 us
    dot_general x8, matrix products, edge_pass(): jnp.einsum('fbc,fcx->fbx', select_bf, dst_high, preferred_element_type=jn...  20 us
    dot_general x8, matrix products, edge_pass(): jnp.einsum('fbc,fdcl->fdbl', select_f32, other_pos, precision=lax.Precisi...  15.5 us
    all_to_all x1, starting transfers between devices, shards(): lax.all_to_all(mean_msg, 'tm', split_axis=1, concat_axis=0, tiled=True)  10.3 us
  transfers between devices with their start and end apart: 6, of which 4 were waited for; matrix products, arithmetic and copies ran while one was open for 7% of the time, Pallas kernels for 0%

commit v1 on v0

v1 whole, which is shorter than its diff:
```python
import math

import jax
import jax.numpy as jnp
import numpy as np
from jax import lax
from jax.experimental import pallas as pl
from jax.experimental.pallas import tpu as pltpu
from jax.sharding import PartitionSpec as P

H = 128
L = 32
G = 6
FR = 16
NB = 14
EXT = NB + 2 * G
S = 8
T = 128
K = 64
PAIRS = 7
LAG = 2
MESH = pl.DeviceIdType.MESH
F32 = jnp.float32
BF = jnp.bfloat16


def dot(a, b):
    return jnp.dot(a, b, preferred_element_type=F32)


def split_np(values):
    import ml_dtypes

    high = values.astype(ml_dtypes.bfloat16)
    low = (values - high.astype(np.float64)).astype(ml_dtypes.bfloat16)
    return high, low


def transforms():
    k = np.arange(K)
    t = np.arange(T)
    angle = 2.0 * math.pi / T * ((k[:, None] * t[None, :]) % T)
    forward = np.concatenate([np.cos(angle), -np.sin(angle)], axis=0)
    fwd = np.concatenate(split_np(forward), axis=0)
    weight = (np.where(k == 0, 1.0, 2.0) / T)[None, :]
    inverse = np.concatenate([np.cos(angle.T) * weight, -np.sin(angle.T) * weight], axis=1)
    inv_hi, inv_lo = split_np(inverse)
    return jnp.asarray(fwd), jnp.asarray(inv_hi), jnp.asarray(inv_lo)


def rows(start, size):
    return pl.ds(pl.multiple_of(start, size), size)


def kernel(
    idx,
    pos3,
    edge_in,
    edge_out,
    edge_params,
    coord_w,
    node_in,
    node_out,
    node_bias,
    fwd,
    inv_hi,
    inv_lo,
    feats_hbm,
    spec_hbm,
    out,
    out_pos,
    ext,
    ghost,
    pt,
    po,
    near,
    scaled,
    acc_buf,
    send_buf,
    recv_buf,
    conv_buf,
    back_buf,
    spec,
    coef,
    mixed,
    node_buf,
    w_src,
    w_dst,
    w_edge,
    w_coord,
    w_n1,
    w_n2,
    loc_sem,
    pos_send,
    pos_recv,
    halo_send,
    halo_recv,
    msg_send,
    msg_recv,
    conv_send,
    conv_recv,
):
    sp = lax.axis_index("space")
    tm = lax.axis_index("tm")
    count = lax.axis_size("space")
    y = tm % 4
    half = tm // 4
    right = (sp + 1) % count
    left = (sp + count - 1) % count

    def partner_y(d):
        if d % 4 == 0:
            return y
        if d % 4 == 1:
            return y + 1 - 2 * (y % 2)
        if d % 4 == 2:
            return (y + 2) % 4
        return 3 - y

    def partner(d):
        return (1 - half if d >= 4 else half) * 4 + partner_y(d)

    barrier = pltpu.get_barrier_semaphore()
    for other in (left, right):
        pl.semaphore_signal(barrier, inc=1, device_id=(other, tm), device_id_type=MESH)
    for d in range(1, 8):
        pl.semaphore_signal(barrier, inc=1, device_id=(sp, partner(d)), device_id_type=MESH)

    own_copy = pltpu.make_async_copy(feats_hbm, ext.at[:, pl.ds(G, NB)], loc_sem.at[0])
    own_copy.start()
    spec_copy = pltpu.make_async_copy(spec_hbm, spec, loc_sem.at[1])
    spec_copy.start()

    group16 = lax.broadcasted_iota(jnp.int32, (FR, 128), 1) // L
    for b in range(NB):
        q, w = b // 4, b % 4
        tile = jnp.zeros((FR, 128), F32)
        for d in range(3):
            part = pos3[d, :, q * 128 : (q + 1) * 128]
            shift = (L * (d - w)) % 128
            if shift:
                part = pltpu.roll(part, shift, 1)
            tile = jnp.where(group16 == d, part, tile)
        pt[G + b] = tile

    pl.semaphore_wait(barrier, 9)

    def pos_copy(side):
        if side == 0:
            src, dst, dev = NB, 0, right
        else:
            src, dst, dev = G, G + NB, left
        return pltpu.make_async_remote_copy(
            src_ref=pt.at[pl.ds(src, G)],
            dst_ref=pt.at[pl.ds(dst, G)],
            send_sem=pos_send.at[side],
            recv_sem=pos_recv.at[side],
            device_id=(dev, tm),
            device_id_type=MESH,
        )

    def halo_copy(side, q):
        if side == 0:
            src, dev = NB - 1 - q, right
        else:
            src, dev = q, left
        return pltpu.make_async_remote_copy(
            src_ref=feats_hbm.at[:, src],
            dst_ref=ghost.at[side, q],
            send_sem=halo_send.at[side, q],
            recv_sem=halo_recv.at[side, q],
            device_id=(dev, tm),
            device_id_type=MESH,
        )

    def msg_copy(j, d):
        return pltpu.make_async_remote_copy(
            src_ref=send_buf.at[j, :, rows(partner_y(d) * 8, 8)],
            dst_ref=recv_buf.at[j, :, :, rows(tm * FR, FR), :],
            send_sem=msg_send.at[j, d - 1],
            recv_sem=msg_recv.at[j, d - 1],
            device_id=(sp, partner(d)),
            device_id_type=MESH,
        )

    def conv_copy(j, d):
        return pltpu.make_async_remote_copy(
            src_ref=conv_buf.at[j, :, :, rows(partner_y(d) * FR, FR), :],
            dst_ref=back_buf.at[j, :, y],
            send_sem=conv_send.at[j, d - 1],
            recv_sem=conv_recv.at[j, d - 1],
            device_id=(sp, partner(d)),
            device_id_type=MESH,
        )

    for side in range(2):
        pos_copy(side).start()
    for q in range(G):
        for side in range(2):
            halo_copy(side, q).start()

    def half_bf(v):
        return (v.astype(F32) * 0.5).astype(BF)

    zero = jnp.zeros((H, H), BF)
    src_half = half_bf(edge_in[:H, :])
    dst_half = half_bf(edge_in[H:, :])
    edge_half = half_bf(edge_out[...])
    row = lax.broadcasted_iota(jnp.int32, (H, H), 0)
    lane = lax.broadcasted_iota(jnp.int32, (H, H), 1)
    bias = edge_params[0:1, :] * 0.5
    dist_w = edge_params[1:2, :] * 0.5

    def split3(v):
        a = v.astype(BF).astype(F32)
        r = v - a
        b = r.astype(BF).astype(F32)
        return a, b, (r - b).astype(BF).astype(F32)

    bias_parts = split3(bias)
    dist_hi, dist_lo, _ = split3(dist_w)
    cw_hi = jnp.broadcast_to(coord_w[...], (H, H)).T
    cw_hi, cw_lo, _ = split3(cw_hi)
    for s in range(S):
        p, c = s // 2, (s % 2) * H
        w_src[p, :H, c : c + H] = src_half
        block = jnp.where((row == s) | (row == 8 + s), dist_hi, 0.0)
        block = jnp.where(row == 16 + s, dist_lo, block)
        for i in range(3):
            block = jnp.where(row == 24 + i, bias_parts[i], block)
        w_src[p, H:, c : c + H] = block.astype(BF)
        w_coord[p, c : c + H, :] = jnp.where(
            lane == s, cw_hi, jnp.where(lane == 8 + s, cw_lo, 0.0)
        ).astype(BF)
    for dst_ref, w in ((w_dst, dst_half), (w_edge, edge_half)):
        dst_ref[:H, :H] = w
        dst_ref[H:, H:] = w
        dst_ref[:H, H:] = zero
        dst_ref[H:, :H] = zero
    w_n1[...] = half_bf(node_in[:H, :])
    w_n2[...] = half_bf(node_in[H:, :])
    edge_bias = edge_params[2:3, :] * 0.5
    edge_bias2 = jnp.concatenate([edge_bias, edge_bias], axis=1)
    node_b0 = node_bias[0:1, :] * 0.5
    node_b1 = node_bias[1:2, :]

    for side in range(2):
        pos_copy(side).wait()
    own_copy.wait()

    group = lax.broadcasted_iota(jnp.int32, (8, 128), 1) // L

    def own_rows(f, b):
        return ext[f, G + b]

    def edge_block(j, e, b):
        def frame_group(fg, carry):
            dist = jnp.zeros((8, 128), F32)
            for u in range(4):
                f = fg * 4 + u
                base = (f * NB + b) * S
                for s in range(S):
                    near[u * 8 + s : u * 8 + s + 1, :] = pt[idx[base + s], pl.ds(f, 1), :]
                own = pt[G + b, pl.ds(f, 1), :]
                offset = own - near[u * 8 : (u + 1) * 8, :]
                square = offset * offset
                square = square + pltpu.roll(square, 64, 1)
                square = square + pltpu.roll(square, 32, 1)
                scaled[u * 8 : (u + 1) * 8, :] = offset / (1.0 + jnp.sqrt(square + 1.0))
                dist = jnp.where(group == u, square, dist)
            d_hi = dist.astype(BF).astype(F32)
            d_lo = (dist - d_hi).astype(BF).astype(F32)
            aug = jnp.concatenate(
                [d_hi, d_lo, d_hi, jnp.ones((8, 128), F32), jnp.zeros((96, 128), F32)], axis=0
            )
            aug = aug.T.astype(BF)
            own_f = jnp.concatenate([own_rows(fg * 4 + u, b) for u in range(4)], axis=0)
            first = jnp.concatenate([own_f, aug], axis=1)
            acc = jnp.zeros((H, H), F32)
            wsum = jnp.zeros((H, H), F32)
            for p in range(4):
                cols = []
                for s in (2 * p, 2 * p + 1):
                    parts = []
                    for u in range(4):
                        f = fg * 4 + u
                        i = idx[(f * NB + b) * S + s]
                        parts.append(ext[f, i])
                    cols.append(jnp.concatenate(parts, axis=0))
                second = jnp.concatenate(cols, axis=1)
                pre = dot(first, w_src[p]) + dot(second, w_dst[...])
                hidden = (pre * jnp.tanh(pre) + pre).astype(BF)
                act = dot(hidden, w_edge[...]) + edge_bias2
                msg = act * jnp.tanh(act) + act
                acc = acc + (msg[:, :H] + msg[:, H:])
                wsum = wsum + dot(msg.astype(BF), w_coord[p])
            acc_buf[rows(fg * 128, 128), :] = acc * (1.0 / S)
            wt = wsum.T
            wv = wt[0:8, :] + wt[8:16, :]
            for u in range(4):
                f = fg * 4 + u
                one = jnp.where(group == u, wv, 0.0)
                one = one + pltpu.roll(one, 64, 1)
                one = one + pltpu.roll(one, 32, 1)
                moved = jnp.sum(scaled[u * 8 : (u + 1) * 8, :] * one, axis=0, keepdims=True)
                own = pt[G + b, pl.ds(f, 1), :]
                po[pl.ds(b * FR + f, 1), :] = own + moved * (1.0 / S)
            return carry

        lax.fori_loop(0, 4, frame_group, 0)
        for l in range(L):
            send_buf[j, e, l] = acc_buf[pl.ds(l, FR, stride=L), :].astype(BF)
        recv_buf[j, e, :, rows(tm * FR, FR), :] = send_buf[j, e, rows(y * 8, 8)]

    def edge_pair(j):
        @pl.when(j >= 1)
        def _():
            q = j - 1
            for side in range(2):
                halo_copy(side, q).wait_recv()
            for f in range(FR):
                ext[f, G - 1 - q] = ghost[0, q, f]
                ext[f, G + NB + q] = ghost[1, q, f]

        edge_block(j, 0, 6 - j)
        edge_block(j, 1, 7 + j)
        for d in (4, 5, 7, 6, 1, 3, 2):
            msg_copy(j, d).start()

    def spectral_pair(j):
        for d in range(1, 8):
            msg_copy(j, d).wait_recv()
        for e in range(2):

            def analyse(r, carry):
                c2 = dot(fwd[...], recv_buf[j, e, r])
                coef[rows((e * 8 + r) * T, T), :] = c2[:T] + c2[T:]
                return carry

            lax.fori_loop(0, 8, analyse, 0)

        def mode(k, carry):
            re = coef[pl.ds(k, 16, stride=T), :].astype(BF)
            im = coef[pl.ds(K + k, 16, stride=T), :].astype(BF)
            lhs = jnp.concatenate(
                [jnp.concatenate([re, -im], axis=1), jnp.concatenate([im, re], axis=1)], axis=0
            )
            w = jnp.concatenate([spec[0, k], spec[1, k]], axis=0)
            m = dot(lhs, w)
            mixed[rows(k * 16, 16), :] = m[:16]
            mixed[rows((K + k) * 16, 16), :] = m[16:]
            return carry

        lax.fori_loop(0, K, mode, 0)
        rows_t = rows(half * 64, 64)
        for e in range(2):

            def synth(r, carry):
                m = mixed[pl.ds(e * 8 + r, T, stride=16), :]
                hi = m.astype(BF)
                lo = (m - hi.astype(F32)).astype(BF)
                ihi = inv_hi[rows_t, :]
                c = dot(ihi, hi) + dot(inv_lo[rows_t, :], hi) + dot(ihi, lo)
                conv_buf[j, e, r] = c.astype(BF)
                return carry

            lax.fori_loop(0, 8, synth, 0)
        for d in (1, 3, 2):
            conv_copy(j, d).start()
        for e in range(2):
            back_buf[j, e, y] = conv_buf[j, e, :, rows(y * FR, FR), :]

    def node_pair(j):
        for d in (1, 3, 2):
            conv_copy(j, d).wait_recv()
        for e in range(2):
            b = 6 - j if e == 0 else 7 + j
            node_buf[...] = dot(back_buf[j, e].reshape(L * FR, H), w_n2[...])

            def frame_group(fg, carry):
                part = jnp.concatenate(
                    [node_buf[pl.ds(fg * 4 + u, L, stride=FR), :] for u in range(4)], axis=0
                )
                own = jnp.concatenate([own_rows(fg * 4 + u, b) for u in range(4)], axis=0)
                pre = dot(own, w_n1[...]) + part + node_b0
                hidden = (pre * jnp.tanh(pre) + pre).astype(BF)
                res = own.astype(F32) + (dot(hidden, node_out[...]) + node_b1)
                res = res.astype(BF)
                for u in range(4):
                    out[fg * 4 + u, rows(b * L, L), :] = res[u * L : (u + 1) * L]
                return carry

            lax.fori_loop(0, 4, frame_group, 0)

    def step(j, carry):
        @pl.when(j < PAIRS)
        def _():
            edge_pair(j)

        @pl.when(j > LAG)
        def _():
            node_pair(j - LAG - 1)

        @pl.when(j == LAG)
        def _():
            spec_copy.wait()

        @pl.when((j >= LAG) & (j < PAIRS + LAG))
        def _():
            spectral_pair(j - LAG)

        return carry

    lax.fori_loop(0, PAIRS + LAG + 1, step, 0)

    for d in range(3):
        for q in range(4):
            tile = jnp.zeros((FR, 128), F32)
            for w in range(4):
                b = q * 4 + w
                if b < NB:
                    part = po[b * FR : (b + 1) * FR, :]
                    shift = (L * (w - d)) % 128
                    if shift:
                        part = pltpu.roll(part, shift, 1)
                    tile = jnp.where(group16 == w, part, tile)
            out_pos[d, :, q * 128 : (q + 1) * 128] = tile

    for side in range(2):
        for q in range(G):
            halo_copy(side, q).wait_send()

    def drain(j, carry):
        for d in range(1, 8):
            msg_copy(j, d).wait_send()
        for d in range(1, 4):
            conv_copy(j, d).wait_send()
        return carry

    lax.fori_loop(0, PAIRS, drain, 0)


def shards(
    node_feats,
    positions,
    neighbours,
    edge_in,
    edge_out,
    edge_params,
    coord_weight,
    spectral,
    node_in,
    node_out,
    node_bias,
):
    first = lax.axis_index("space") * NB - G
    total = NB * lax.axis_size("space")
    idx = ((neighbours - first) % total).reshape(-1)
    pos3 = jnp.pad(jnp.transpose(positions, (1, 0, 2)), ((0, 0), (0, 0), (0, 64)))
    fwd, inv_hi, inv_lo = transforms()
    vmem = pl.BlockSpec(memory_space=pltpu.VMEM)
    hbm = pl.BlockSpec(memory_space=pl.ANY)
    dma = pltpu.SemaphoreType.DMA
    new_feats, pos_out = pl.pallas_call(
        kernel,
        out_shape=(
            jax.ShapeDtypeStruct((FR, NB * L, H), BF),
            jax.ShapeDtypeStruct((3, FR, 512), F32),
        ),
        in_specs=[pl.BlockSpec(memory_space=pltpu.SMEM)] + [vmem] * 11 + [hbm] * 2,
        out_specs=(vmem, vmem),
        scratch_shapes=[
            pltpu.VMEM((FR, EXT, L, H), BF),
            pltpu.VMEM((2, G, FR, L, H), BF),
            pltpu.VMEM((EXT, FR, 128), F32),
            pltpu.VMEM((NB * FR, 128), F32),
            pltpu.VMEM((32, 128), F32),
            pltpu.VMEM((32, 128), F32),
            pltpu.VMEM((FR * L, H), F32),
            pltpu.VMEM((PAIRS, 2, L, FR, H), BF),
            pltpu.VMEM((PAIRS, 2, 8, T, H), BF),
            pltpu.VMEM((PAIRS, 2, 8, 64, H), BF),
            pltpu.VMEM((PAIRS, 2, 4, 8, FR, H), BF),
            pltpu.VMEM((2, K, H, H), BF),
            pltpu.VMEM((16 * T, H), F32),
            pltpu.VMEM((16 * T, H), F32),
            pltpu.VMEM((FR * L, H), F32),
            pltpu.VMEM((4, 2 * H, 2 * H), BF),
            pltpu.VMEM((2 * H, 2 * H), BF),
            pltpu.VMEM((2 * H, 2 * H), BF),
            pltpu.VMEM((4, 2 * H, H), BF),
            pltpu.VMEM((H, H), BF),
            pltpu.VMEM((H, H), BF),
            dma((2,)),
            dma((2,)),
            dma((2,)),
            dma((2, G)),
            dma((2, G)),
            dma((PAIRS, 7)),
            dma((PAIRS, 7)),
            dma((PAIRS, 3)),
            dma((PAIRS, 3)),
        ],
        compiler_params=pltpu.CompilerParams(
            collective_id=0, has_side_effects=True, vmem_limit_bytes=56 * 1024 * 1024
        ),
    )(
        idx,
        pos3,
        edge_in,
        edge_out,
        edge_params,
        coord_weight.reshape(1, H),
        node_in,
        node_out,
        node_bias,
        fwd,
        inv_hi,
        inv_lo,
        node_feats.reshape(FR, NB, L, H),
        spectral,
    )
    new_positions = jnp.transpose(pos_out, (1, 0, 2))[:, :, : NB * L]
    return (new_feats, new_positions)


def solution(mesh):
    placed = (
        P("tm", "space", None),
        P("tm", None, "space"),
        P("tm", "space", None),
        P(),
        P(),
        P(),
        P(),
        P(),
        P(),
        P(),
        P(),
    )
    return jax.shard_map(
        shards,
        mesh=mesh,
        in_specs=placed,
        out_specs=(P("tm", "space", None), P("tm", None, "space")),
        check_vma=False,
    )
```

time: 353 us -> 248 us (0.70); the launches traced: 347 us -> 247 us
  Pallas kernels: 0 us -> 239 us
  matrix products: 150 us -> 0 us
  waiting for transfers between devices: 98.3 us -> 0 us
  local copies, waits for them, and re-layouts: 67.2 us -> 5.89 us
  starting transfers between devices: 18.7 us -> 0 us
  other arithmetic: 11.2 us -> 0.86 us
    pallas_call x0 -> x1, Pallas kernels: none -> 239 us  [shards(): pl.pallas_call(kernel, out_shape=(jax.ShapeDtypeStruct((FR, NB * L, H), B...]
    dot_general x45 -> x0, matrix products: 150 us -> none  [the longest x8 46.9 us: edge_pass(): jnp.einsum('fbc,fcx->fbx', select_bf, dst_low, preferred_element_type=jnp...]
    all_to_all x2 -> x0, waiting for transfers between devices: 87.1 us -> none  [the longest x1 46.1 us: shards(): lax.all_to_all(mean_msg, 'tm', split_axis=1, concat_axis=0, tiled=True)]
    reshape x12 -> x1, local copies, waits for them, and re-layouts: 45.3 us -> 0.7 us  [shards(): idx = ((neighbours - first) % total).reshape(-1)]
    all_to_all x2 -> x0, starting transfers between devices: 15.1 us -> none  [the longest x1 10.3 us: shards(): lax.all_to_all(mean_msg, 'tm', split_axis=1, concat_axis=0, tiled=True)]
    ppermute x4 -> x0, waiting for transfers between devices: 11.2 us -> none  [the longest x2 8.19 us: with_halo(): lax.ppermute(lax.slice_in_dim(block, block.shape[dim] - width, None, axis...]
    convert_element_type x2 -> x0, other arithmetic: 9.04 us -> none  [the longest x1 8.14 us: split_parts(): low_part = (values - high_part.astype(jnp.float32)).astype(jnp.bfloat16)]
    another operation x1 -> x0, local copies, waits for them, and re-layouts: 8.48 us -> none  [edge_pass(): flat_dst = other_dst.reshape(frames, other_blocks, block_len * feat_width)]
  transfers between devices with their start and end apart: 6 -> 0, of which waited for: 4 -> 0; matrix products, arithmetic and copies ran while one was open for 7% -> 0% of each run, Pallas kernels for 0% -> 0%
where the time goes in v1:
time: 248 us; the launch traced here: 247 us
  Pallas kernels  239 us (96%)
  local copies, waits for them, and re-layouts  5.89 us (2%)
    pallas_call x1, Pallas kernels, shards(): pl.pallas_call(kernel, out_shape=(jax.ShapeDtypeStruct((FR, NB * L, H), B...  239 us

profile of v1, /device:TPU:38, one launch (start us, length us, event | category | flops | bytes accessed | tf_op | source)
XLA Modules:
  0.0 246.8 jit_solution(2711698835469380133)
XLA Ops:
  0.6 0.9 add_select_fusion
  1.5 0.1 copy.16
  1.6 0.7 reshape.13.idx
  2.3 1.5 pad.4.pos3
  3.9 239.4 %shard_map.149 = (bf16[16,448,128]{2,1,0:T(8,128)(2,1)}, f32[3,16,512]{2,1,0:T(8,128)}) custom-call(s32[1792]{0:T(1024)} %reshape.13.idx, f32[3,16,512]{2,1,0:T(8,128)} %pad.4.pos3, bf16[256,128]{1,0:T(8,128)(2,1)} %edge_in.1, bf16[128,128]{1,0:T(8,128)(2,1)} %edge_out.1, f32[3,128]{1,0:T(4,128)} %edge_params.1, f32[1,128]{1,0:T(1,128)} %bitcast.8, ...), custom_call_target="tpu_custom_call" | custom-call | tf_op jit(solution)/shard_map/pallas_call | solution.py:464
  243.3 0.0 copy-start
  243.3 2.9 %copy.19 = bf16[16,448,128]{2,1,0:T(8,128)(2,1)} copy(bf16[16,448,128]{2,1,0:T(8,128)(2,1)} %get-tuple-element.8) | data formatting | bytes 3670016
  246.2 0.0 copy-done
  246.2 0.6 copy.20
Async XLA Ops:
  243.3 2.9 %copy-start = (f32[3,16,512]{2,1,0:T(8,128)S(1)}, f32[3,16,512]{2,1,0:T(8,128)}, u32[]{:S(2)}) copy-start(f32[3,16,512]{2,1,0:T(8,128)} %get-tuple-element.5) | copy-start | bytes 294916

commit v2 on v1

--- a/solution.py
+++ b/solution.py
@@ -250,64 +250,63 @@
 
     group = lax.broadcasted_iota(jnp.int32, (8, 128), 1) // L
 
-    def own_rows(f, b):
-        return ext[f, G + b]
+    def own_all(b):
+        return jnp.concatenate([ext[f, G + b] for f in range(FR)], axis=0)
 
     def edge_block(j, e, b):
-        def frame_group(fg, carry):
+        augs = []
+        for h in range(4):
             dist = jnp.zeros((8, 128), F32)
             for u in range(4):
-                f = fg * 4 + u
+                f = h * 4 + u
                 base = (f * NB + b) * S
                 for s in range(S):
-                    near[u * 8 + s : u * 8 + s + 1, :] = pt[idx[base + s], pl.ds(f, 1), :]
-                own = pt[G + b, pl.ds(f, 1), :]
-                offset = own - near[u * 8 : (u + 1) * 8, :]
+                    near[f * 8 + s : f * 8 + s + 1, :] = pt[idx[base + s], f : f + 1, :]
+                own = pt[G + b, f : f + 1, :]
+                offset = own - near[f * 8 : (f + 1) * 8, :]
                 square = offset * offset
                 square = square + pltpu.roll(square, 64, 1)
                 square = square + pltpu.roll(square, 32, 1)
-                scaled[u * 8 : (u + 1) * 8, :] = offset / (1.0 + jnp.sqrt(square + 1.0))
+                scaled[f * 8 : (f + 1) * 8, :] = offset / (1.0 + jnp.sqrt(square + 1.0))
                 dist = jnp.where(group == u, square, dist)
             d_hi = dist.astype(BF).astype(F32)
             d_lo = (dist - d_hi).astype(BF).astype(F32)
             aug = jnp.concatenate(
                 [d_hi, d_lo, d_hi, jnp.ones((8, 128), F32), jnp.zeros((96, 128), F32)], axis=0
             )
-            aug = aug.T.astype(BF)
-            own_f = jnp.concatenate([own_rows(fg * 4 + u, b) for u in range(4)], axis=0)
-            first = jnp.concatenate([own_f, aug], axis=1)
-            acc = jnp.zeros((H, H), F32)
-            wsum = jnp.zeros((H, H), F32)
-            for p in range(4):
-                cols = []
-                for s in (2 * p, 2 * p + 1):
-                    parts = []
-                    for u in range(4):
-                        f = fg * 4 + u
-                        i = idx[(f * NB + b) * S + s]
-                        parts.append(ext[f, i])
-                    cols.append(jnp.concatenate(parts, axis=0))
-                second = jnp.concatenate(cols, axis=1)
-                pre = dot(first, w_src[p]) + dot(second, w_dst[...])
-                hidden = (pre * jnp.tanh(pre) + pre).astype(BF)
-                act = dot(hidden, w_edge[...]) + edge_bias2
-                msg = act * jnp.tanh(act) + act
-                acc = acc + (msg[:, :H] + msg[:, H:])
-                wsum = wsum + dot(msg.astype(BF), w_coord[p])
-            acc_buf[rows(fg * 128, 128), :] = acc * (1.0 / S)
-            wt = wsum.T
+            augs.append(aug.T.astype(BF))
+        first = jnp.concatenate([own_all(b), jnp.concatenate(augs, axis=0)], axis=1)
+        acc = None
+        wsum = None
+        for p in range(4):
+            cols = []
+            for s in (2 * p, 2 * p + 1):
+                cols.append(
+                    jnp.concatenate(
+                        [ext[f, idx[(f * NB + b) * S + s]] for f in range(FR)], axis=0
+                    )
+                )
+            second = jnp.concatenate(cols, axis=1)
+            pre = dot(first, w_src[p]) + dot(second, w_dst[...])
+            hidden = (pre * jnp.tanh(pre) + pre).astype(BF)
+            act = dot(hidden, w_edge[...]) + edge_bias2
+            msg = act * jnp.tanh(act) + act
+            both = msg[:, :H] + msg[:, H:]
+            part = dot(msg.astype(BF), w_coord[p])
+            acc = both if p == 0 else acc + both
+            wsum = part if p == 0 else wsum + part
+        acc_buf[...] = acc * (1.0 / S)
+        for h in range(4):
+            wt = wsum[h * 128 : (h + 1) * 128, :].T
             wv = wt[0:8, :] + wt[8:16, :]
             for u in range(4):
-                f = fg * 4 + u
+                f = h * 4 + u
                 one = jnp.where(group == u, wv, 0.0)
                 one = one + pltpu.roll(one, 64, 1)
                 one = one + pltpu.roll(one, 32, 1)
-                moved = jnp.sum(scaled[u * 8 : (u + 1) * 8, :] * one, axis=0, keepdims=True)
-                own = pt[G + b, pl.ds(f, 1), :]
+                moved = jnp.sum(scaled[f * 8 : (f + 1) * 8, :] * one, axis=0, keepdims=True)
+                own = pt[G + b, f : f + 1, :]
                 po[pl.ds(b * FR + f, 1), :] = own + moved * (1.0 / S)
-            return carry
-
-        lax.fori_loop(0, 4, frame_group, 0)
         for l in range(L):
             send_buf[j, e, l] = acc_buf[pl.ds(l, FR, stride=L), :].astype(BF)
         recv_buf[j, e, :, rows(tm * FR, FR), :] = send_buf[j, e, rows(y * 8, 8)]
@@ -332,12 +331,18 @@
             msg_copy(j, d).wait_recv()
         for e in range(2):
 
-            def analyse(r, carry):
-                c2 = dot(fwd[...], recv_buf[j, e, r])
-                coef[rows((e * 8 + r) * T, T), :] = c2[:T] + c2[T:]
+            def analyse(i, carry):
+                r = 2 * i
+                c2 = dot(
+                    fwd[...],
+                    jnp.concatenate([recv_buf[j, e, r], recv_buf[j, e, r + 1]], axis=1),
+                )
+                c = c2[:T] + c2[T:]
+                coef[rows((e * 8 + r) * T, T), :] = c[:, :H]
+                coef[rows((e * 8 + r + 1) * T, T), :] = c[:, H:]
                 return carry
 
-            lax.fori_loop(0, 8, analyse, 0)
+            lax.fori_loop(0, 4, analyse, 0, unroll=True)
 
         def mode(k, carry):
             re = coef[pl.ds(k, 16, stride=T), :].astype(BF)
@@ -351,20 +356,25 @@
             mixed[rows((K + k) * 16, 16), :] = m[16:]
             return carry
 
-        lax.fori_loop(0, K, mode, 0)
+        lax.fori_loop(0, K, mode, 0, unroll=8)
         rows_t = rows(half * 64, 64)
+        inv = jnp.concatenate([inv_hi[rows_t, :], inv_lo[rows_t, :]], axis=0)
         for e in range(2):
 
-            def synth(r, carry):
-                m = mixed[pl.ds(e * 8 + r, T, stride=16), :]
+            def synth(i, carry):
+                r = 2 * i
+                m = jnp.concatenate(
+                    [mixed[pl.ds(e * 8 + r + n, T, stride=16), :] for n in range(2)], axis=1
+                )
                 hi = m.astype(BF)
                 lo = (m - hi.astype(F32)).astype(BF)
-                ihi = inv_hi[rows_t, :]
-                c = dot(ihi, hi) + dot(inv_lo[rows_t, :], hi) + dot(ihi, lo)
-                conv_buf[j, e, r] = c.astype(BF)
+                c2 = dot(inv, hi)
+                c = (c2[:64] + c2[64:] + dot(inv[:64], lo)).astype(BF)
+                conv_buf[j, e, r] = c[:, :H]
+                conv_buf[j, e, r + 1] = c[:, H:]
                 return carry
 
-            lax.fori_loop(0, 8, synth, 0)
+            lax.fori_loop(0, 4, synth, 0, unroll=True)
         for d in (1, 3, 2):
             conv_copy(j, d).start()
         for e in range(2):
@@ -376,21 +386,16 @@
         for e in range(2):
             b = 6 - j if e == 0 else 7 + j
             node_buf[...] = dot(back_buf[j, e].reshape(L * FR, H), w_n2[...])
-
-            def frame_group(fg, carry):
-                part = jnp.concatenate(
-                    [node_buf[pl.ds(fg * 4 + u, L, stride=FR), :] for u in range(4)], axis=0
-                )
-                own = jnp.concatenate([own_rows(fg * 4 + u, b) for u in range(4)], axis=0)
-                pre = dot(own, w_n1[...]) + part + node_b0
-                hidden = (pre * jnp.tanh(pre) + pre).astype(BF)
-                res = own.astype(F32) + (dot(hidden, node_out[...]) + node_b1)
-                res = res.astype(BF)
-                for u in range(4):
-                    out[fg * 4 + u, rows(b * L, L), :] = res[u * L : (u + 1) * L]
-                return carry
-
-            lax.fori_loop(0, 4, frame_group, 0)
+            part = jnp.concatenate(
+                [node_buf[pl.ds(f, L, stride=FR), :] for f in range(FR)], axis=0
+            )
+            own = own_all(b)
+            pre = dot(own, w_n1[...]) + part + node_b0
+            hidden = (pre * jnp.tanh(pre) + pre).astype(BF)
+            res = own.astype(F32) + (dot(hidden, node_out[...]) + node_b1)
+            res = res.astype(BF)
+            for f in range(FR):
+                out[f, rows(b * L, L), :] = res[f * L : (f + 1) * L]
 
     def step(j, carry):
         @pl.when(j < PAIRS)
@@ -474,8 +479,8 @@
             pltpu.VMEM((2, G, FR, L, H), BF),
             pltpu.VMEM((EXT, FR, 128), F32),
             pltpu.VMEM((NB * FR, 128), F32),
-            pltpu.VMEM((32, 128), F32),
-            pltpu.VMEM((32, 128), F32),
+            pltpu.VMEM((FR * S, 128), F32),
+            pltpu.VMEM((FR * S, 128), F32),
             pltpu.VMEM((FR * L, H), F32),
             pltpu.VMEM((PAIRS, 2, L, FR, H), BF),
             pltpu.VMEM((PAIRS, 2, 8, T, H), BF),

time: 248 us -> 148 us (0.60)
  Pallas kernels: 239 us -> 139 us
    pallas_call x1, Pallas kernels: 239 us -> 139 us  [shards(): pl.pallas_call(kernel, out_shape=(jax.ShapeDtypeStruct((FR, NB * L, H), B...]
where the time goes in v2:
time: 148 us; the launch traced here: 146 us
  Pallas kernels  139 us (94%)
  local copies, waits for them, and re-layouts  5.89 us (4%)
    pallas_call x1, Pallas kernels, shards(): pl.pallas_call(kernel, out_shape=(jax.ShapeDtypeStruct((FR, NB * L, H), B...  139 us
    unnamed x4, local copies, waits for them, and re-layouts  3.54 us

profile of v2, /device:TPU:38, one launch (start us, length us, event | category | flops | bytes accessed | tf_op | source)
XLA Modules:
  0.0 146.3 jit_solution(957656587230756992)
XLA Ops:
  0.6 0.9 add_select_fusion
  1.5 0.1 copy.16
  1.6 0.7 reshape.13.idx
  2.3 1.5 %pad.4.pos3 = f32[3,16,512]{2,1,0:T(8,128)} pad(f32[3,16,448]{2,1,0:T(8,128)} %bitcast.6, f32[]{:T(128)} %constant.31.clone.1), padding=0_0x0_0x0_64 | pad | bytes 184324 | tf_op jit(solution)/shard_map/jit(_pad)/pad | solution.py:464
  3.9 138.9 %shard_map.149 = (bf16[16,448,128]{2,1,0:T(8,128)(2,1)}, f32[3,16,512]{2,1,0:T(8,128)}) custom-call(s32[1792]{0:T(1024)} %reshape.13.idx, f32[3,16,512]{2,1,0:T(8,128)} %pad.4.pos3, bf16[256,128]{1,0:T(8,128)(2,1)} %edge_in.1, bf16[128,128]{1,0:T(8,128)(2,1)} %edge_out.1, f32[3,128]{1,0:T(4,128)} %edge_params.1, f32[1,128]{1,0:T(1,128)} %bitcast.8, ...), custom_call_target="tpu_custom_call" | custom-call | tf_op jit(solution)/shard_map/pallas_call | solution.py:469
  142.8 0.0 copy-start
  142.8 2.9 %copy.19 = bf16[16,448,128]{2,1,0:T(8,128)(2,1)} copy(bf16[16,448,128]{2,1,0:T(8,128)(2,1)} %get-tuple-element.8) | data formatting | bytes 3670016
  145.7 0.0 copy-done
  145.7 0.6 copy.20
Async XLA Ops:
  142.8 2.9 %copy-start = (f32[3,16,512]{2,1,0:T(8,128)S(1)}, f32[3,16,512]{2,1,0:T(8,128)}, u32[]{:S(2)}) copy-start(f32[3,16,512]{2,1,0:T(8,128)} %get-tuple-element.5) | copy-start | bytes 294916

commit v3 on v2

--- a/solution.py
+++ b/solution.py
@@ -18,7 +18,7 @@
 T = 128
 K = 64
 PAIRS = 7
-LAG = 2
+LAG = 1
 MESH = pl.DeviceIdType.MESH
 F32 = jnp.float32
 BF = jnp.bfloat16
@@ -71,6 +71,7 @@
     out_pos,
     ext,
     ghost,
+    pos_ghost,
     pt,
     po,
     near,
@@ -105,6 +106,8 @@
     count = lax.axis_size("space")
     y = tm % 4
     half = tm // 4
+    total = NB * count
+    first_block = sp * NB - G
     right = (sp + 1) % count
     left = (sp + count - 1) % count
 
@@ -131,28 +134,16 @@
     spec_copy = pltpu.make_async_copy(spec_hbm, spec, loc_sem.at[1])
     spec_copy.start()
 
-    group16 = lax.broadcasted_iota(jnp.int32, (FR, 128), 1) // L
-    for b in range(NB):
-        q, w = b // 4, b % 4
-        tile = jnp.zeros((FR, 128), F32)
-        for d in range(3):
-            part = pos3[d, :, q * 128 : (q + 1) * 128]
-            shift = (L * (d - w)) % 128
-            if shift:
-                part = pltpu.roll(part, shift, 1)
-            tile = jnp.where(group16 == d, part, tile)
-        pt[G + b] = tile
-
     pl.semaphore_wait(barrier, 9)
 
     def pos_copy(side):
         if side == 0:
-            src, dst, dev = NB, 0, right
+            src, dev = NB, right
         else:
-            src, dst, dev = G, G + NB, left
+            src, dev = G, left
         return pltpu.make_async_remote_copy(
             src_ref=pt.at[pl.ds(src, G)],
-            dst_ref=pt.at[pl.ds(dst, G)],
+            dst_ref=pos_ghost.at[side],
             send_sem=pos_send.at[side],
             recv_sem=pos_recv.at[side],
             device_id=(dev, tm),
@@ -193,11 +184,29 @@
             device_id_type=MESH,
         )
 
-    for side in range(2):
-        pos_copy(side).start()
     for q in range(G):
         for side in range(2):
             halo_copy(side, q).start()
+
+    group16 = lax.broadcasted_iota(jnp.int32, (FR, 128), 1) // L
+    for b in range(NB):
+        q, w = b // 4, b % 4
+        tile = jnp.zeros((FR, 128), F32)
+        for d in range(3):
+            if q < 3:
+                part = pos3[d, :, q * 128 : (q + 1) * 128]
+            else:
+                part = jnp.concatenate(
+                    [pos3[d, :, 384:448], jnp.zeros((FR, 64), F32)], axis=1
+                )
+            shift = (L * (d - w)) % 128
+            if shift:
+                part = pltpu.roll(part, shift, 1)
+            tile = jnp.where(group16 == d, part, tile)
+        pt[G + b] = tile
+
+    for side in range(2):
+        pos_copy(side).start()
 
     def half_bf(v):
         return (v.astype(F32) * 0.5).astype(BF)
@@ -244,8 +253,6 @@
     node_b0 = node_bias[0:1, :] * 0.5
     node_b1 = node_bias[1:2, :]
 
-    for side in range(2):
-        pos_copy(side).wait()
     own_copy.wait()
 
     group = lax.broadcasted_iota(jnp.int32, (8, 128), 1) // L
@@ -254,14 +261,20 @@
         return jnp.concatenate([ext[f, G + b] for f in range(FR)], axis=0)
 
     def edge_block(j, e, b):
+        picked = {}
+        for f in range(FR):
+            for s in range(S):
+                v = idx[b, s, f] - first_block
+                v = jnp.where(v < 0, v + total, v)
+                v = jnp.where(v >= total, v - total, v)
+                picked[f, s] = jnp.minimum(v, EXT - 1)
         augs = []
         for h in range(4):
             dist = jnp.zeros((8, 128), F32)
             for u in range(4):
                 f = h * 4 + u
-                base = (f * NB + b) * S
                 for s in range(S):
-                    near[f * 8 + s : f * 8 + s + 1, :] = pt[idx[base + s], f : f + 1, :]
+                    near[f * 8 + s : f * 8 + s + 1, :] = pt[picked[f, s], f : f + 1, :]
                 own = pt[G + b, f : f + 1, :]
                 offset = own - near[f * 8 : (f + 1) * 8, :]
                 square = offset * offset
@@ -283,7 +296,7 @@
             for s in (2 * p, 2 * p + 1):
                 cols.append(
                     jnp.concatenate(
-                        [ext[f, idx[(f * NB + b) * S + s]] for f in range(FR)], axis=0
+                        [ext[f, picked[f, s]] for f in range(FR)], axis=0
                     )
                 )
             second = jnp.concatenate(cols, axis=1)
@@ -312,6 +325,13 @@
         recv_buf[j, e, :, rows(tm * FR, FR), :] = send_buf[j, e, rows(y * 8, 8)]
 
     def edge_pair(j):
+        @pl.when(j == 1)
+        def _():
+            for side in range(2):
+                pos_copy(side).wait()
+            pt[:G] = pos_ghost[0]
+            pt[G + NB :] = pos_ghost[1]
+
         @pl.when(j >= 1)
         def _():
             q = j - 1
@@ -429,7 +449,8 @@
                     if shift:
                         part = pltpu.roll(part, shift, 1)
                     tile = jnp.where(group16 == w, part, tile)
-            out_pos[d, :, q * 128 : (q + 1) * 128] = tile
+            width = min(128, NB * L - q * 128)
+            out_pos[d, :, q * 128 : q * 128 + width] = tile[:, :width]
 
     for side in range(2):
         for q in range(G):
@@ -458,10 +479,8 @@
     node_out,
     node_bias,
 ):
-    first = lax.axis_index("space") * NB - G
-    total = NB * lax.axis_size("space")
-    idx = ((neighbours - first) % total).reshape(-1)
-    pos3 = jnp.pad(jnp.transpose(positions, (1, 0, 2)), ((0, 0), (0, 0), (0, 64)))
+    idx = jnp.transpose(neighbours, (1, 2, 0))
+    pos3 = jnp.transpose(positions, (1, 0, 2))
     fwd, inv_hi, inv_lo = transforms()
     vmem = pl.BlockSpec(memory_space=pltpu.VMEM)
     hbm = pl.BlockSpec(memory_space=pl.ANY)
@@ -469,14 +488,15 @@
     new_feats, pos_out = pl.pallas_call(
         kernel,
         out_shape=(
-            jax.ShapeDtypeStruct((FR, NB * L, H), BF),
-            jax.ShapeDtypeStruct((3, FR, 512), F32),
+            pltpu.VMEM((FR, NB * L, H), BF),
+            pltpu.VMEM((3, FR, NB * L), F32),
         ),
         in_specs=[pl.BlockSpec(memory_space=pltpu.SMEM)] + [vmem] * 11 + [hbm] * 2,
         out_specs=(vmem, vmem),
         scratch_shapes=[
             pltpu.VMEM((FR, EXT, L, H), BF),
             pltpu.VMEM((2, G, FR, L, H), BF),
+            pltpu.VMEM((2, G, FR, 128), F32),
             pltpu.VMEM((EXT, FR, 128), F32),
             pltpu.VMEM((NB * FR, 128), F32),
             pltpu.VMEM((FR * S, 128), F32),
@@ -525,7 +545,7 @@
         node_feats.reshape(FR, NB, L, H),
         spectral,
     )
-    new_positions = jnp.transpose(pos_out, (1, 0, 2))[:, :, : NB * L]
+    new_positions = jnp.transpose(pos_out, (1, 0, 2))
     return (new_feats, new_positions)
 
 

time: 148 us -> 141 us (0.953)
  the two profiles are of different devices: /device:TPU:38 before, /device:TPU:30 now
where the time goes in v3:
time: 141 us
  Pallas kernels  138 us (98%)
  local copies, waits for them, and re-layouts  1.87 us (1%)
    pallas_call x1, Pallas kernels, shards(): pl.pallas_call(kernel, out_shape=(pltpu.VMEM((FR, NB * L, H), BF), pltpu....  138 us

profile of v3, /device:TPU:30, one launch (start us, length us, event | category | flops | bytes accessed | tf_op | source)
XLA Modules:
  0.0 140.9 jit_solution(3733477174555286464)
XLA Ops:
  0.6 138.4 %shard_map.149 = (bf16[16,448,128]{2,1,0:T(8,128)(2,1)S(1)}, f32[3,16,448]{2,1,0:T(8,128)S(1)}) custom-call(s32[14,8,16]{2,1,0:T(8,128)} %bitcast.8, f32[3,16,448]{2,1,0:T(8,128)} %bitcast.7, bf16[256,128]{1,0:T(8,128)(2,1)} %edge_in.1, bf16[128,128]{1,0:T(8,128)(2,1)} %edge_out.1, f32[3,128]{1,0:T(4,128)} %edge_params.1, f32[1,128]{1,0:T(1,128)} %bitcast.9, ...), custom_call_target="tpu_custom_call" | custom-call | tf_op jit(solution)/shard_map/pallas_call | solution.py:488
  139.0 1.2 copy.18
  140.3 0.6 copy.19

commit v4 on v3

--- a/solution.py
+++ b/solution.py
@@ -164,22 +164,22 @@
             device_id_type=MESH,
         )
 
-    def msg_copy(j, d):
+    def msg_copy(j, e, d):
         return pltpu.make_async_remote_copy(
-            src_ref=send_buf.at[j, :, rows(partner_y(d) * 8, 8)],
-            dst_ref=recv_buf.at[j, :, :, rows(tm * FR, FR), :],
-            send_sem=msg_send.at[j, d - 1],
-            recv_sem=msg_recv.at[j, d - 1],
+            src_ref=send_buf.at[j, e, rows(partner_y(d) * 8, 8)],
+            dst_ref=recv_buf.at[j, e, :, rows(tm * FR, FR), :],
+            send_sem=msg_send.at[j, e, d - 1],
+            recv_sem=msg_recv.at[j, e, d - 1],
             device_id=(sp, partner(d)),
             device_id_type=MESH,
         )
 
-    def conv_copy(j, d):
+    def conv_copy(j, e, d):
         return pltpu.make_async_remote_copy(
-            src_ref=conv_buf.at[j, :, :, rows(partner_y(d) * FR, FR), :],
-            dst_ref=back_buf.at[j, :, y],
-            send_sem=conv_send.at[j, d - 1],
-            recv_sem=conv_recv.at[j, d - 1],
+            src_ref=conv_buf.at[j, e, :, rows(partner_y(d) * FR, FR), :],
+            dst_ref=back_buf.at[j, e, y],
+            send_sem=conv_send.at[j, e, d - 1],
+            recv_sem=conv_recv.at[j, e, d - 1],
             device_id=(sp, partner(d)),
             device_id_type=MESH,
         )
@@ -341,50 +341,45 @@
                 ext[f, G - 1 - q] = ghost[0, q, f]
                 ext[f, G + NB + q] = ghost[1, q, f]
 
-        edge_block(j, 0, 6 - j)
-        edge_block(j, 1, 7 + j)
-        for d in (4, 5, 7, 6, 1, 3, 2):
-            msg_copy(j, d).start()
-
-    def spectral_pair(j):
-        for d in range(1, 8):
-            msg_copy(j, d).wait_recv()
         for e in range(2):
-
-            def analyse(i, carry):
-                r = 2 * i
+            edge_block(j, e, 6 - j if e == 0 else 7 + j)
+            for d in (4, 5, 7, 6, 1, 3, 2):
+                msg_copy(j, e, d).start()
+
+    def spectral_part(j, blocks):
+        n = 8 * len(blocks)
+        for i, e in enumerate(blocks):
+            for d in range(1, 8):
+                msg_copy(j, e, d).wait_recv()
+            for r in range(0, 8, 2):
                 c2 = dot(
                     fwd[...],
                     jnp.concatenate([recv_buf[j, e, r], recv_buf[j, e, r + 1]], axis=1),
                 )
                 c = c2[:T] + c2[T:]
-                coef[rows((e * 8 + r) * T, T), :] = c[:, :H]
-                coef[rows((e * 8 + r + 1) * T, T), :] = c[:, H:]
-                return carry
-
-            lax.fori_loop(0, 4, analyse, 0, unroll=True)
+                at = (i * 8 + r) * T
+                coef[at : at + T, :] = c[:, :H]
+                coef[at + T : at + 2 * T, :] = c[:, H:]
 
         def mode(k, carry):
-            re = coef[pl.ds(k, 16, stride=T), :].astype(BF)
-            im = coef[pl.ds(K + k, 16, stride=T), :].astype(BF)
+            re = coef[pl.ds(k, n, stride=T), :]
+            im = coef[pl.ds(K + k, n, stride=T), :]
             lhs = jnp.concatenate(
                 [jnp.concatenate([re, -im], axis=1), jnp.concatenate([im, re], axis=1)], axis=0
-            )
+            ).astype(BF)
             w = jnp.concatenate([spec[0, k], spec[1, k]], axis=0)
             m = dot(lhs, w)
-            mixed[rows(k * 16, 16), :] = m[:16]
-            mixed[rows((K + k) * 16, 16), :] = m[16:]
+            mixed[rows(k * n, n), :] = m[:n]
+            mixed[rows((K + k) * n, n), :] = m[n:]
             return carry
 
         lax.fori_loop(0, K, mode, 0, unroll=8)
         rows_t = rows(half * 64, 64)
         inv = jnp.concatenate([inv_hi[rows_t, :], inv_lo[rows_t, :]], axis=0)
-        for e in range(2):
-
-            def synth(i, carry):
-                r = 2 * i
+        for i, e in enumerate(blocks):
+            for r in range(0, 8, 2):
                 m = jnp.concatenate(
-                    [mixed[pl.ds(e * 8 + r + n, T, stride=16), :] for n in range(2)], axis=1
+                    [mixed[pl.ds(i * 8 + r + v, T, stride=n), :] for v in range(2)], axis=1
                 )
                 hi = m.astype(BF)
                 lo = (m - hi.astype(F32)).astype(BF)
@@ -392,19 +387,15 @@
                 c = (c2[:64] + c2[64:] + dot(inv[:64], lo)).astype(BF)
                 conv_buf[j, e, r] = c[:, :H]
                 conv_buf[j, e, r + 1] = c[:, H:]
-                return carry
-
-            lax.fori_loop(0, 4, synth, 0, unroll=True)
-        for d in (1, 3, 2):
-            conv_copy(j, d).start()
-        for e in range(2):
+            for d in (2, 1, 3):
+                conv_copy(j, e, d).start()
             back_buf[j, e, y] = conv_buf[j, e, :, rows(y * FR, FR), :]
 
     def node_pair(j):
-        for d in (1, 3, 2):
-            conv_copy(j, d).wait_recv()
         for e in range(2):
             b = 6 - j if e == 0 else 7 + j
+            for d in (1, 3, 2):
+                conv_copy(j, e, d).wait_recv()
             node_buf[...] = dot(back_buf[j, e].reshape(L * FR, H), w_n2[...])
             part = jnp.concatenate(
                 [node_buf[pl.ds(f, L, stride=FR), :] for f in range(FR)], axis=0
@@ -417,6 +408,33 @@
             for f in range(FR):
                 out[f, rows(b * L, L), :] = res[f * L : (f + 1) * L]
 
+    def close_sends(j, carry):
+        for e in range(2):
+            for d in range(1, 8):
+                msg_copy(j, e, d).wait_send()
+            for d in range(1, 4):
+                conv_copy(j, e, d).wait_send()
+        return carry
+
+    def before_last():
+        for d in range(3):
+            for q in range(4):
+                tile = jnp.zeros((FR, 128), F32)
+                for w in range(4):
+                    b = q * 4 + w
+                    if b < NB:
+                        part = po[b * FR : (b + 1) * FR, :]
+                        shift = (L * (w - d)) % 128
+                        if shift:
+                            part = pltpu.roll(part, shift, 1)
+                        tile = jnp.where(group16 == w, part, tile)
+                width = min(128, NB * L - q * 128)
+                out_pos[d, :, q * 128 : q * 128 + width] = tile[:, :width]
+        for side in range(2):
+            for q in range(G):
+                halo_copy(side, q).wait_send()
+        lax.fori_loop(0, PAIRS - 2, close_sends, 0)
+
     def step(j, carry):
         @pl.when(j < PAIRS)
         def _():
@@ -430,40 +448,20 @@
         def _():
             spec_copy.wait()
 
-        @pl.when((j >= LAG) & (j < PAIRS + LAG))
+        @pl.when((j >= LAG) & (j < PAIRS + LAG - 1))
         def _():
-            spectral_pair(j - LAG)
+            spectral_part(j - LAG, (0, 1))
 
         return carry
 
-    lax.fori_loop(0, PAIRS + LAG + 1, step, 0)
-
-    for d in range(3):
-        for q in range(4):
-            tile = jnp.zeros((FR, 128), F32)
-            for w in range(4):
-                b = q * 4 + w
-                if b < NB:
-                    part = po[b * FR : (b + 1) * FR, :]
-                    shift = (L * (w - d)) % 128
-                    if shift:
-                        part = pltpu.roll(part, shift, 1)
-                    tile = jnp.where(group16 == w, part, tile)
-            width = min(128, NB * L - q * 128)
-            out_pos[d, :, q * 128 : q * 128 + width] = tile[:, :width]
-
-    for side in range(2):
-        for q in range(G):
-            halo_copy(side, q).wait_send()
-
-    def drain(j, carry):
-        for d in range(1, 8):
-            msg_copy(j, d).wait_send()
-        for d in range(1, 4):
-            conv_copy(j, d).wait_send()
-        return carry
-
-    lax.fori_loop(0, PAIRS, drain, 0)
+    lax.fori_loop(0, PAIRS + LAG - 1, step, 0)
+    last = PAIRS - 1
+    node_pair(last - 1)
+    before_last()
+    spectral_part(last, (0,))
+    spectral_part(last, (1,))
+    node_pair(last)
+    lax.fori_loop(PAIRS - 2, PAIRS, close_sends, 0)
 
 
 def shards(
@@ -521,10 +519,10 @@
             dma((2,)),
             dma((2, G)),
             dma((2, G)),
-            dma((PAIRS, 7)),
-            dma((PAIRS, 7)),
-            dma((PAIRS, 3)),
-            dma((PAIRS, 3)),
+            dma((PAIRS, 2, 7)),
+            dma((PAIRS, 2, 7)),
+            dma((PAIRS, 2, 3)),
+            dma((PAIRS, 2, 3)),
         ],
         compiler_params=pltpu.CompilerParams(
             collective_id=0, has_side_effects=True, vmem_limit_bytes=56 * 1024 * 1024

time: 141 us -> 141 us (level)
  the two profiles are of different devices: /device:TPU:30 before, /device:TPU:6 now
where the time goes in v4:
time: 141 us
  Pallas kernels  138 us (98%)
  local copies, waits for them, and re-layouts  1.87 us (1%)
    pallas_call x1, Pallas kernels, shards(): pl.pallas_call(kernel, out_shape=(pltpu.VMEM((FR, NB * L, H), BF), pltpu....  138 us

profile of v4, /device:TPU:6, one launch (start us, length us, event | category | flops | bytes accessed | tf_op | source)
XLA Modules:
  0.0 140.8 jit_solution(7544589348197326397)
XLA Ops:
  0.6 138.3 %shard_map.149 = (bf16[16,448,128]{2,1,0:T(8,128)(2,1)S(1)}, f32[3,16,448]{2,1,0:T(8,128)S(1)}) custom-call(s32[14,8,16]{2,1,0:T(8,128)} %bitcast.8, f32[3,16,448]{2,1,0:T(8,128)} %bitcast.7, bf16[256,128]{1,0:T(8,128)(2,1)} %edge_in.1, bf16[128,128]{1,0:T(8,128)(2,1)} %edge_out.1, f32[3,128]{1,0:T(4,128)} %edge_params.1, f32[1,128]{1,0:T(1,128)} %bitcast.9, ...), custom_call_target="tpu_custom_call" | custom-call | tf_op jit(solution)/shard_map/pallas_call | solution.py:486
  138.9 1.2 copy.18
  140.2 0.6 copy.19

commit v5 on v4

--- a/solution.py
+++ b/solution.py
@@ -184,9 +184,8 @@
             device_id_type=MESH,
         )
 
-    for q in range(G):
-        for side in range(2):
-            halo_copy(side, q).start()
+    for side in range(2):
+        halo_copy(side, 0).start()
 
     group16 = lax.broadcasted_iota(jnp.int32, (FR, 128), 1) // L
     for b in range(NB):
@@ -207,6 +206,9 @@
 
     for side in range(2):
         pos_copy(side).start()
+    for q in range(1, G):
+        for side in range(2):
+            halo_copy(side, q).start()
 
     def half_bf(v):
         return (v.astype(F32) * 0.5).astype(BF)
@@ -329,6 +331,9 @@
         def _():
             for side in range(2):
                 pos_copy(side).wait()
+            for e in range(2):
+                for d in (4, 5, 7, 6, 1, 3, 2):
+                    msg_copy(0, e, d).start()
             pt[:G] = pos_ghost[0]
             pt[G + NB :] = pos_ghost[1]
 
@@ -343,8 +348,10 @@
 
         for e in range(2):
             edge_block(j, e, 6 - j if e == 0 else 7 + j)
-            for d in (4, 5, 7, 6, 1, 3, 2):
-                msg_copy(j, e, d).start()
+            @pl.when(j > 0)
+            def _():
+                for d in (4, 5, 7, 6, 1, 3, 2):
+                    msg_copy(j, e, d).start()
 
     def spectral_part(j, blocks):
         n = 8 * len(blocks)

time: 141 us -> 136 us (0.965)
  the two profiles are of different devices: /device:TPU:6 before, /device:TPU:38 now
where the time goes in v5:
time: 136 us
  Pallas kernels  134 us (99%)
  local copies, waits for them, and re-layouts  1.87 us (1%)
    pallas_call x1, Pallas kernels, shards(): pl.pallas_call(kernel, out_shape=(pltpu.VMEM((FR, NB * L, H), BF), pltpu....  134 us

profile of v5, /device:TPU:38, one launch (start us, length us, event | category | flops | bytes accessed | tf_op | source)
XLA Modules:
  0.0 136.3 jit_solution(7503911511178379550)
XLA Ops:
  0.6 133.8 %shard_map.149 = (bf16[16,448,128]{2,1,0:T(8,128)(2,1)S(1)}, f32[3,16,448]{2,1,0:T(8,128)S(1)}) custom-call(s32[14,8,16]{2,1,0:T(8,128)} %bitcast.8, f32[3,16,448]{2,1,0:T(8,128)} %bitcast.7, bf16[256,128]{1,0:T(8,128)(2,1)} %edge_in.1, bf16[128,128]{1,0:T(8,128)(2,1)} %edge_out.1, f32[3,128]{1,0:T(4,128)} %edge_params.1, f32[1,128]{1,0:T(1,128)} %bitcast.9, ...), custom_call_target="tpu_custom_call" | custom-call | tf_op jit(solution)/shard_map/pallas_call | solution.py:493
  134.4 1.2 copy.18
  135.6 0.6 copy.19

commit v6 on v5

--- a/solution.py
+++ b/solution.py
@@ -331,9 +331,6 @@
         def _():
             for side in range(2):
                 pos_copy(side).wait()
-            for e in range(2):
-                for d in (4, 5, 7, 6, 1, 3, 2):
-                    msg_copy(0, e, d).start()
             pt[:G] = pos_ghost[0]
             pt[G + NB :] = pos_ghost[1]
 
@@ -345,6 +342,12 @@
             for f in range(FR):
                 ext[f, G - 1 - q] = ghost[0, q, f]
                 ext[f, G + NB + q] = ghost[1, q, f]
+
+        @pl.when(j == 1)
+        def _():
+            for e in range(2):
+                for d in (4, 5, 7, 6, 1, 3, 2):
+                    msg_copy(0, e, d).start()
 
         for e in range(2):
             edge_block(j, e, 6 - j if e == 0 else 7 + j)

time: 136 us -> 136 us (level)
  no operation moved by 1% of the time
where the time goes in v6:
time: 136 us
  Pallas kernels  134 us (99%)
  local copies, waits for them, and re-layouts  1.87 us (1%)
    pallas_call x1, Pallas kernels, shards(): pl.pallas_call(kernel, out_shape=(pltpu.VMEM((FR, NB * L, H), BF), pltpu....  134 us

profile of v6, /device:TPU:38, one launch (start us, length us, event | category | flops | bytes accessed | tf_op | source)
XLA Modules:
  0.0 136.3 jit_solution(10525548740766787708)
XLA Ops:
  0.6 133.8 %shard_map.149 = (bf16[16,448,128]{2,1,0:T(8,128)(2,1)S(1)}, f32[3,16,448]{2,1,0:T(8,128)S(1)}) custom-call(s32[14,8,16]{2,1,0:T(8,128)} %bitcast.8, f32[3,16,448]{2,1,0:T(8,128)} %bitcast.7, bf16[256,128]{1,0:T(8,128)(2,1)} %edge_in.1, bf16[128,128]{1,0:T(8,128)(2,1)} %edge_out.1, f32[3,128]{1,0:T(4,128)} %edge_params.1, f32[1,128]{1,0:T(1,128)} %bitcast.9, ...), custom_call_target="tpu_custom_call" | custom-call | tf_op jit(solution)/shard_map/pallas_call | solution.py:496
  134.4 1.2 copy.18
  135.6 0.6 copy.19
